TPU v7x, 128 devices: a whole 4x4x4 slice. The times are simulated.
128 devices in a mesh: grid: 16 (over y, x_hi, core), head: 8 (over x_lo, z).
Axes of the slice: x: 4 (x_hi: 2, x_lo: 2; x = x_hi * 2 + x_lo), y: 4, z: 4, core: 2. Of those that a mesh axis runs over, the one named last changes fastest.
Arguments:
- queries: bfloat16 [65536, 1024], P('grid', 'head'), may hold values from -12 to 12
- resid: bfloat16 [65536, 1024], P('grid', 'head'), may hold values from -6 to 6
- keys: bfloat16 [98304, 1024], P('grid', 'head'), may hold values from -6 to 6
- values: bfloat16 [98304, 1024], P('grid', 'head'), may hold values from -6 to 6
- w_out: bfloat16 [1024, 1024], replicated, may hold values from -0.75 to 0.75
- block_lists: int32 [512, 12], P('grid'), may hold values from 0 to 767, as said below
- block_counts: int32 [512], P('grid'), may hold values from 1 to 12, as said below
Outputs:
- mixed: bfloat16 [65536, 1024], P('grid', 'head')
Inputs may be any that keep to these rules, and one draw needn't show every extreme that they name: `block_lists`: each row lists 12 different latent blocks. The blocks listed for grid blocks of the g-th 4096 grid points lie in latent blocks (g - 1) * 48 to (g + 2) * 48 - 1. `block_counts`: entries of a list at positions not below the count are not used.
All inputs are finite; a program needn't handle non-finite values.
Results may differ from a plain program's by a relative error of at most 0.005.
Values may be sent and summed in bfloat16 or wider, within the bound.
A program may use at most 128 MiB of HBM per device.

v0:
```python
import math

import jax
import jax.numpy as jnp
from jax import lax
from jax.sharding import PartitionSpec as P

D = 1024
HEADS = 16
BLK = 128


def extended(cells, sides, width):
    for axis, dim in sides:
        count = lax.axis_size(axis)
        ends = count - 1
        head = lax.slice_in_dim(cells, 0, width, axis=dim)
        tail = lax.slice_in_dim(cells, cells.shape[dim] - width, cells.shape[dim], axis=dim)
        cells = jnp.concatenate(
            [
                lax.ppermute(tail, axis, [(i, (i + 1) % count) for i in range(ends)]),
                cells,
                lax.ppermute(head, axis, [((i + 1) % count, i) for i in range(ends)]),
            ],
            axis=dim,
        )
    return cells


def attend(queries, source, first_block, block_lists, block_counts):
    rows, width = queries.shape
    head_dim = D // HEADS
    heads_here = width // head_dim
    scale = 1.0 / math.sqrt(head_dim)
    slots = block_lists.shape[1]
    group = 4
    tiles = source.reshape(2, source.shape[1] // BLK, BLK, width)
    local_ids = block_lists - first_block
    live = jnp.arange(slots, dtype=jnp.int32)[None, :] < block_counts[:, None]
    query_groups = queries.reshape(-1, group, BLK, width)
    id_groups = local_ids.reshape(-1, group, slots)
    live_groups = live.reshape(-1, group, slots)
    column_head = jnp.arange(width, dtype=jnp.int32) // head_dim
    head_masks = column_head[None, :] == jnp.arange(heads_here, dtype=jnp.int32)[:, None]
    masks_low = head_masks.astype(jnp.bfloat16)
    masks_float = head_masks.astype(jnp.float32)

    def one_group(packed):
        block_q, block_ids, block_live = packed
        block_k = tiles[0][block_ids].reshape(group, slots * BLK, width)
        block_v = tiles[1][block_ids].reshape(group, slots * BLK, width)
        usable = jnp.broadcast_to(block_live[:, :, None], (group, slots, BLK)).reshape(
            group, slots * BLK
        )
        masked_q = block_q[:, None, :, :] * masks_low[None, :, None, :]
        score = (
            jnp.einsum("ghqc,gkc->ghqk", masked_q, block_k, preferred_element_type=jnp.float32)
            * scale
        )
        score = jnp.where(usable[:, None, None, :], score, -1e30)
        top = jnp.max(score, axis=-1, keepdims=True)
        weight = jnp.exp(score - top)
        total = jnp.sum(weight, axis=-1, keepdims=True)
        weight_low = weight.astype(jnp.bfloat16)
        summed = jnp.einsum(
            "ghqk,gkc->ghqc", weight_low, block_v, preferred_element_type=jnp.float32
        )
        summed = jnp.sum(summed / total * masks_float[None, :, None, :], axis=1)
        return summed.astype(jnp.bfloat16).reshape(group * BLK, width)

    attended = lax.map(one_group, (query_groups, id_groups, live_groups))
    return attended.reshape(rows, width)


def local(queries, resid, keys, values, w_out, block_lists, block_counts):
    owned = jnp.stack((keys, values))
    per_device = keys.shape[0] // BLK
    source = extended(owned, (("grid", 1),), keys.shape[0])
    first_block = (lax.axis_index("grid") - 1) * per_device
    attended = attend(queries, source, first_block, block_lists, block_counts)
    arrived, resid_rows = (
        lax.all_to_all(attended, "head", split_axis=0, concat_axis=1, tiled=True),
        lax.all_to_all(resid, "head", split_axis=0, concat_axis=1, tiled=True),
    )
    projected = jnp.dot(arrived, w_out, preferred_element_type=jnp.float32)
    mixed_rows = (resid_rows.astype(jnp.float32) + projected).astype(jnp.bfloat16)
    return lax.all_to_all(mixed_rows, "head", split_axis=1, concat_axis=0, tiled=True)


def solution(mesh):
    placed = (
        P("grid", "head"),
        P("grid", "head"),
        P("grid", "head"),
        P("grid", "head"),
        P(),
        P("grid", None),
        P("grid"),
    )
    return jax.shard_map(
        local, mesh=mesh, in_specs=placed, out_specs=P("grid", "head"), check_vma=False
    )
```

profile of v0, /device:TPU:24, one launch (start us, length us, event | category | flops | bytes accessed | tf_op | source)
XLA Modules:
  0.0 353.2 jit_solution(9857969000131741715)
XLA Ops:
  4.0 4.5 %collective-permute-start.1 = (bf16[2,6144,128]{2,1,0:T(8,128)(2,1)}, bf16[2,6144,128]{2,1,0:T(8,128)(2,1)}, u32[]{:S(2)}, u32[]{:S(2)}) collective-permute-start(bf16[2,6144,128]{2,1,0:T(8,128)(2,1)} %pad_maximum_fusion.1), channel_id=1, source_target_pairs={{8,0},{16,8},{24,16},{32,24},{40,32},{48,40},{56,48},{64,56},{72,6... | collective-permute-start | bytes 9437192 | tf_op jit(solution)/shard_map/ppermute | solution.py:23
  10.5 5.4 %all-to-all-start = ((bf16[8,512,128]{2,1,0:T(8,128)(2,1)}), bf16[8,512,128]{2,1,0:T(8,128)(2,1)S(1)}, u32[]{:S(2)}, u32[]{:S(2)}) async-start(bf16[8,512,128]{2,1,0:T(8,128)(2,1)} %bitcast), calls=%async_computation | async-start | bytes 2097152 | tf_op jit(solution)/shard_map/all_to_all | solution.py:83
  16.1 59.4 %collective-permute-done.1 = bf16[2,6144,128]{2,1,0:T(8,128)(2,1)} collective-permute-done((bf16[2,6144,128]{2,1,0:T(8,128)(2,1)}, bf16[2,6144,128]{2,1,0:T(8,128)(2,1)}, u32[]{:S(2)}, u32[]{:S(2)}) %collective-permute-start.1) | collective-permute-done | bytes 3145760 | tf_op jit(solution)/shard_map/ppermute | solution.py:23
  75.5 8.1 %collective-permute-done = bf16[2,6144,128]{2,1,0:T(8,128)(2,1)} collective-permute-done((bf16[2,6144,128]{2,1,0:T(8,128)(2,1)}, bf16[2,6144,128]{2,1,0:T(8,128)(2,1)}, u32[]{:S(2)}, u32[]{:S(2)}) %collective-permute-start) | collective-permute-done | bytes 3145760 | tf_op jit(solution)/shard_map/ppermute | solution.py:21
  83.6 11.6 %pad_maximum_fusion = bf16[2,18432,128]{2,1,0:T(8,128)(2,1)} fusion(bf16[2,6144,128]{2,1,0:T(8,128)(2,1)} %collective-permute-done.1, bf16[1,6144,128]{2,1,0:T(8,128)(2,1)} %bitcast.85, bf16[1,6144,128]{2,1,0:T(8,128)(2,1)} %bitcast.87, bf16[2,6144,128]{2,1,0:T(8,128)(2,1)} %collective-permute-done), kind=kLoop, calls=%fused_computation.32 | loop fusion | flops 37748736 | bytes 18874368 | tf_op jit(solution)/shard_map/concatenate | solution.py:19
  95.2 223.7 %while.12 = (s32[]{:T(128)}, bf16[8,512,128]{1,2,0:T(8,128)(2,1)}, pred[8,4,12]{2,1,0:T(4,128)(4,1)S(1)}, bf16[8,4,128,128]{3,2,1,0:T(8,128)(2,1)}, bf16[2,144,1...) while((s32[]{:T(128)}, bf16[8,512,128]{1,2,0:T(8,128)(2,1)}, ...), condition=%wide.region_4.5_spmd.clone.clone, body=%wide.region_0.4_spmd.clone.clone.sunk | while | flops 823066496 | bytes 54592600 | solution.py:71
  95.2 11.7 %slice_bitcast_fusion.3 = (bf16[144,128,128]{2,1,0:T(8,128)(2,1)}, bf16[144,128,128]{2,1,0:T(8,128)(2,1)}) fusion(bf16[2,144,128,128]{3,2,1,0:T(8,128)(2,1)} %get-tuple-element.183), kind=kLoop, calls=%fused_computation.10.clone.1 | loop fusion | bytes 18874368 | tf_op jit(solution)/shard_map/while/body/eval_jaxpr/squeeze | solution.py:50
  107.0 4.3 %gather_fusion = bf16[48,128,128]{2,1,0:T(8,128)(2,1)} fusion(bf16[144,128,128]{2,1,0:T(8,128)(2,1)} %get-tuple-element.157, s32[1024]{0:T(1024)S(1)} %pad_clamp_fusion.2), kind=kCustom, calls=%fused_computation.1.clone.clone.clone.1 | custom fusion | bytes 3145920 | tf_op jit(solution)/shard_map/while/body/eval_jaxpr/gather | solution.py:51
  111.4 4.3 %gather_fusion.1 = bf16[48,128,128]{2,1,0:T(8,128)(2,1)} fusion(bf16[144,128,128]{2,1,0:T(8,128)(2,1)} %get-tuple-element.158, s32[1024]{0:T(1024)S(1)} %pad_clamp_fusion.2), kind=kCustom, calls=%fused_computation.clone.clone.clone.1 | custom fusion | bytes 3145920 | tf_op jit(solution)/shard_map/while/body/eval_jaxpr/gather | solution.py:50
  123.2 11.7 %slice_bitcast_fusion.3 = (bf16[144,128,128]{2,1,0:T(8,128)(2,1)}, bf16[144,128,128]{2,1,0:T(8,128)(2,1)}) fusion(bf16[2,144,128,128]{3,2,1,0:T(8,128)(2,1)} %get-tuple-element.183), kind=kLoop, calls=%fused_computation.10.clone.1 | loop fusion | bytes 18874368 | tf_op jit(solution)/shard_map/while/body/eval_jaxpr/squeeze | solution.py:50
  135.0 4.3 %gather_fusion = bf16[48,128,128]{2,1,0:T(8,128)(2,1)} fusion(bf16[144,128,128]{2,1,0:T(8,128)(2,1)} %get-tuple-element.157, s32[1024]{0:T(1024)S(1)} %pad_clamp_fusion.2), kind=kCustom, calls=%fused_computation.1.clone.clone.clone.1 | custom fusion | bytes 3145920 | tf_op jit(solution)/shard_map/while/body/eval_jaxpr/gather | solution.py:51
  139.4 4.3 %gather_fusion.1 = bf16[48,128,128]{2,1,0:T(8,128)(2,1)} fusion(bf16[144,128,128]{2,1,0:T(8,128)(2,1)} %get-tuple-element.158, s32[1024]{0:T(1024)S(1)} %pad_clamp_fusion.2), kind=kCustom, calls=%fused_computation.clone.clone.clone.1 | custom fusion | bytes 3145920 | tf_op jit(solution)/shard_map/while/body/eval_jaxpr/gather | solution.py:50
  151.2 11.7 %slice_bitcast_fusion.3 = (bf16[144,128,128]{2,1,0:T(8,128)(2,1)}, bf16[144,128,128]{2,1,0:T(8,128)(2,1)}) fusion(bf16[2,144,128,128]{3,2,1,0:T(8,128)(2,1)} %get-tuple-element.183), kind=kLoop, calls=%fused_computation.10.clone.1 | loop fusion | bytes 18874368 | tf_op jit(solution)/shard_map/while/body/eval_jaxpr/squeeze | solution.py:50
  162.9 4.3 %gather_fusion = bf16[48,128,128]{2,1,0:T(8,128)(2,1)} fusion(bf16[144,128,128]{2,1,0:T(8,128)(2,1)} %get-tuple-element.157, s32[1024]{0:T(1024)S(1)} %pad_clamp_fusion.2), kind=kCustom, calls=%fused_computation.1.clone.clone.clone.1 | custom fusion | bytes 3145920 | tf_op jit(solution)/shard_map/while/body/eval_jaxpr/gather | solution.py:51
  167.3 4.3 %gather_fusion.1 = bf16[48,128,128]{2,1,0:T(8,128)(2,1)} fusion(bf16[144,128,128]{2,1,0:T(8,128)(2,1)} %get-tuple-element.158, s32[1024]{0:T(1024)S(1)} %pad_clamp_fusion.2), kind=kCustom, calls=%fused_computation.clone.clone.clone.1 | custom fusion | bytes 3145920 | tf_op jit(solution)/shard_map/while/body/eval_jaxpr/gather | solution.py:50
  179.1 11.7 %slice_bitcast_fusion.3 = (bf16[144,128,128]{2,1,0:T(8,128)(2,1)}, bf16[144,128,128]{2,1,0:T(8,128)(2,1)}) fusion(bf16[2,144,128,128]{3,2,1,0:T(8,128)(2,1)} %get-tuple-element.183), kind=kLoop, calls=%fused_computation.10.clone.1 | loop fusion | bytes 18874368 | tf_op jit(solution)/shard_map/while/body/eval_jaxpr/squeeze | solution.py:50
  190.9 4.3 %gather_fusion = bf16[48,128,128]{2,1,0:T(8,128)(2,1)} fusion(bf16[144,128,128]{2,1,0:T(8,128)(2,1)} %get-tuple-element.157, s32[1024]{0:T(1024)S(1)} %pad_clamp_fusion.2), kind=kCustom, calls=%fused_computation.1.clone.clone.clone.1 | custom fusion | bytes 3145920 | tf_op jit(solution)/shard_map/while/body/eval_jaxpr/gather | solution.py:51
  195.3 4.3 %gather_fusion.1 = bf16[48,128,128]{2,1,0:T(8,128)(2,1)} fusion(bf16[144,128,128]{2,1,0:T(8,128)(2,1)} %get-tuple-element.158, s32[1024]{0:T(1024)S(1)} %pad_clamp_fusion.2), kind=kCustom, calls=%fused_computation.clone.clone.clone.1 | custom fusion | bytes 3145920 | tf_op jit(solution)/shard_map/while/body/eval_jaxpr/gather | solution.py:50
  207.1 11.7 %slice_bitcast_fusion.3 = (bf16[144,128,128]{2,1,0:T(8,128)(2,1)}, bf16[144,128,128]{2,1,0:T(8,128)(2,1)}) fusion(bf16[2,144,128,128]{3,2,1,0:T(8,128)(2,1)} %get-tuple-element.183), kind=kLoop, calls=%fused_computation.10.clone.1 | loop fusion | bytes 18874368 | tf_op jit(solution)/shard_map/while/body/eval_jaxpr/squeeze | solution.py:50
  218.9 4.3 %gather_fusion = bf16[48,128,128]{2,1,0:T(8,128)(2,1)} fusion(bf16[144,128,128]{2,1,0:T(8,128)(2,1)} %get-tuple-element.157, s32[1024]{0:T(1024)S(1)} %pad_clamp_fusion.2), kind=kCustom, calls=%fused_computation.1.clone.clone.clone.1 | custom fusion | bytes 3145920 | tf_op jit(solution)/shard_map/while/body/eval_jaxpr/gather | solution.py:51
  223.3 4.3 %gather_fusion.1 = bf16[48,128,128]{2,1,0:T(8,128)(2,1)} fusion(bf16[144,128,128]{2,1,0:T(8,128)(2,1)} %get-tuple-element.158, s32[1024]{0:T(1024)S(1)} %pad_clamp_fusion.2), kind=kCustom, calls=%fused_computation.clone.clone.clone.1 | custom fusion | bytes 3145920 | tf_op jit(solution)/shard_map/while/body/eval_jaxpr/gather | solution.py:50
  235.1 11.7 %slice_bitcast_fusion.3 = (bf16[144,128,128]{2,1,0:T(8,128)(2,1)}, bf16[144,128,128]{2,1,0:T(8,128)(2,1)}) fusion(bf16[2,144,128,128]{3,2,1,0:T(8,128)(2,1)} %get-tuple-element.183), kind=kLoop, calls=%fused_computation.10.clone.1 | loop fusion | bytes 18874368 | tf_op jit(solution)/shard_map/while/body/eval_jaxpr/squeeze | solution.py:50
  246.8 4.3 %gather_fusion = bf16[48,128,128]{2,1,0:T(8,128)(2,1)} fusion(bf16[144,128,128]{2,1,0:T(8,128)(2,1)} %get-tuple-element.157, s32[1024]{0:T(1024)S(1)} %pad_clamp_fusion.2), kind=kCustom, calls=%fused_computation.1.clone.clone.clone.1 | custom fusion | bytes 3145920 | tf_op jit(solution)/shard_map/while/body/eval_jaxpr/gather | solution.py:51
  251.2 4.3 %gather_fusion.1 = bf16[48,128,128]{2,1,0:T(8,128)(2,1)} fusion(bf16[144,128,128]{2,1,0:T(8,128)(2,1)} %get-tuple-element.158, s32[1024]{0:T(1024)S(1)} %pad_clamp_fusion.2), kind=kCustom, calls=%fused_computation.clone.clone.clone.1 | custom fusion | bytes 3145920 | tf_op jit(solution)/shard_map/while/body/eval_jaxpr/gather | solution.py:50
  263.0 11.7 %slice_bitcast_fusion.3 = (bf16[144,128,128]{2,1,0:T(8,128)(2,1)}, bf16[144,128,128]{2,1,0:T(8,128)(2,1)}) fusion(bf16[2,144,128,128]{3,2,1,0:T(8,128)(2,1)} %get-tuple-element.183), kind=kLoop, calls=%fused_computation.10.clone.1 | loop fusion | bytes 18874368 | tf_op jit(solution)/shard_map/while/body/eval_jaxpr/squeeze | solution.py:50
  274.8 4.3 %gather_fusion = bf16[48,128,128]{2,1,0:T(8,128)(2,1)} fusion(bf16[144,128,128]{2,1,0:T(8,128)(2,1)} %get-tuple-element.157, s32[1024]{0:T(1024)S(1)} %pad_clamp_fusion.2), kind=kCustom, calls=%fused_computation.1.clone.clone.clone.1 | custom fusion | bytes 3145920 | tf_op jit(solution)/shard_map/while/body/eval_jaxpr/gather | solution.py:51
  279.2 4.3 %gather_fusion.1 = bf16[48,128,128]{2,1,0:T(8,128)(2,1)} fusion(bf16[144,128,128]{2,1,0:T(8,128)(2,1)} %get-tuple-element.158, s32[1024]{0:T(1024)S(1)} %pad_clamp_fusion.2), kind=kCustom, calls=%fused_computation.clone.clone.clone.1 | custom fusion | bytes 3145920 | tf_op jit(solution)/shard_map/while/body/eval_jaxpr/gather | solution.py:50
  291.0 11.7 %slice_bitcast_fusion.3 = (bf16[144,128,128]{2,1,0:T(8,128)(2,1)}, bf16[144,128,128]{2,1,0:T(8,128)(2,1)}) fusion(bf16[2,144,128,128]{3,2,1,0:T(8,128)(2,1)} %get-tuple-element.183), kind=kLoop, calls=%fused_computation.10.clone.1 | loop fusion | bytes 18874368 | tf_op jit(solution)/shard_map/while/body/eval_jaxpr/squeeze | solution.py:50
  302.8 4.3 %gather_fusion = bf16[48,128,128]{2,1,0:T(8,128)(2,1)} fusion(bf16[144,128,128]{2,1,0:T(8,128)(2,1)} %get-tuple-element.157, s32[1024]{0:T(1024)S(1)} %pad_clamp_fusion.2), kind=kCustom, calls=%fused_computation.1.clone.clone.clone.1 | custom fusion | bytes 3145920 | tf_op jit(solution)/shard_map/while/body/eval_jaxpr/gather | solution.py:51
  307.2 4.3 %gather_fusion.1 = bf16[48,128,128]{2,1,0:T(8,128)(2,1)} fusion(bf16[144,128,128]{2,1,0:T(8,128)(2,1)} %get-tuple-element.158, s32[1024]{0:T(1024)S(1)} %pad_clamp_fusion.2), kind=kCustom, calls=%fused_computation.clone.clone.clone.1 | custom fusion | bytes 3145920 | tf_op jit(solution)/shard_map/while/body/eval_jaxpr/gather | solution.py:50
  319.0 17.6 %all_to_all.48 = bf16[8,512,128]{1,2,0:T(8,128)(2,1)S(1)} all-to-all(bf16[8,512,128]{1,2,0:T(8,128)(2,1)} %get-tuple-element.47), channel_id=1, replica_groups=mesh['grid'=16,'head'=8] {'head'}, dimensions={0} | all-to-all | bytes 2097152 | tf_op jit(solution)/shard_map/all_to_all | solution.py:82
  338.1 14.1 %all_to_all.49 = bf16[512,8,128]{2,0,1:T(8,128)(2,1)S(1)} all-to-all(bf16[512,8,128]{2,0,1:T(8,128)(2,1)S(1)} %bitcast.91), channel_id=1, replica_groups=mesh['grid'=16,'head'=8] {'head'}, dimensions={1} | all-to-all | bytes 2097152 | tf_op jit(solution)/shard_map/all_to_all | solution.py:87
  (138 shorter events, 70.0 us)
Async XLA Ops:
  0.0 336.6 %copy-start = (bf16[1024,1024]{1,0:T(8,128)(2,1)S(1)}, bf16[1024,1024]{1,0:T(8,128)(2,1)}, u32[]{:S(2)}) copy-start(bf16[1024,1024]{1,0:T(8,128)(2,1)} %param.13) | copy-start | bytes 6291460
  0.0 15.8 %copy-start.3 = (s32[32]{0:T(128)S(1)}, s32[32]{0:T(128)}, u32[]{:S(2)}) copy-start(s32[32]{0:T(128)} %param.15) | copy-start | bytes 388
  0.0 15.9 %copy-start.2 = (s32[32,12]{0,1:T(8,128)S(1)}, s32[32,12]{0,1:T(8,128)}, u32[]{:S(2)}) copy-start(s32[32,12]{0,1:T(8,128)} %param.14) | copy-start | bytes 4612
  4.0 71.5 %collective-permute-start.1 = (bf16[2,6144,128]{2,1,0:T(8,128)(2,1)}, bf16[2,6144,128]{2,1,0:T(8,128)(2,1)}, u32[]{:S(2)}, u32[]{:S(2)}) collective-permute-start(bf16[2,6144,128]{2,1,0:T(8,128)(2,1)} %pad_maximum_fusion.1), channel_id=1, source_target_pairs={{8,0},{16,8},{24,16},{32,24},{40,32},{48,40},{56,48},{64,56},{72,6... | collective-permute-start | bytes 9437192 | tf_op jit(solution)/shard_map/ppermute | solution.py:23
  8.5 75.1 %collective-permute-start = (bf16[2,6144,128]{2,1,0:T(8,128)(2,1)}, bf16[2,6144,128]{2,1,0:T(8,128)(2,1)}, u32[]{:S(2)}, u32[]{:S(2)}) collective-permute-start(bf16[2,6144,128]{2,1,0:T(8,128)(2,1)} %pad_maximum_fusion.1), channel_id=1, source_target_pairs={{0,8},{8,16},{16,24},{24,32},{32,40},{40,48},{48,56},{56,64},{64,7... | collective-permute-start | bytes 9437192 | tf_op jit(solution)/shard_map/ppermute | solution.py:21
  10.5 308.5 %all-to-all-start = ((bf16[8,512,128]{2,1,0:T(8,128)(2,1)}), bf16[8,512,128]{2,1,0:T(8,128)(2,1)S(1)}, u32[]{:S(2)}, u32[]{:S(2)}) async-start(bf16[8,512,128]{2,1,0:T(8,128)(2,1)} %bitcast), calls=%async_computation | async-start | bytes 2097152 | tf_op jit(solution)/shard_map/all_to_all | solution.py:83
  119.1 1.4 copy-start.1
  147.1 1.4 copy-start.1
  175.0 1.4 copy-start.1
  203.0 1.4 copy-start.1
  231.0 1.4 copy-start.1
  258.9 1.4 copy-start.1
  286.9 1.4 copy-start.1
  314.9 1.4 copy-start.1
where the time goes:
time: 358 us; the launch traced here: 353 us
  local copies, waits for them, and re-layouts  179 us (50%)
  waiting for transfers between devices  67.5 us (19%)
  matrix products  36.3 us (10%)
  blocking collectives  31.7 us (9%)
  other arithmetic  26.8 us (7%)
  starting transfers between devices  11.8 us (3%)
    squeeze x8, local copies, waits for them, and re-layouts, one_group(): block_k = tiles[0][block_ids].reshape(group, slots * BLK, width)  93.4 us
    ppermute x1, waiting for transfers between devices, extended(): lax.ppermute(head, axis, [((i + 1) % count, i) for i in range(ends)])  59.4 us
    gather x8, local copies, waits for them, and re-layouts, one_group(): block_v = tiles[1][block_ids].reshape(group, slots * BLK, width)  34.4 us
    gather x8, local copies, waits for them, and re-layouts, one_group(): block_k = tiles[0][block_ids].reshape(group, slots * BLK, width)  34.3 us
    dot_general x8, matrix products, one_group(): jnp.einsum('ghqc,gkc->ghqk', masked_q, block_k, preferred_element_type=jn...  19.9 us
    all_to_all x1, blocking collectives, local(): lax.all_to_all(attended, 'head', split_axis=0, concat_axis=1, tiled=True)  17.6 us
    dot_general x8, matrix products, one_group(): jnp.einsum('ghqk,gkc->ghqc', weight_low, block_v, preferred_element_type=...  15.1 us
    all_to_all x1, blocking collectives, local(): lax.all_to_all(mixed_rows, 'head', split_axis=1, concat_axis=0, tiled=True)  14.1 us
  transfers between devices with their start and end apart: 3, of which 2 were waited for; matrix products, arithmetic and copies ran while one was open for 67% of the time, Pallas kernels for 0%

commit v1 on v0

v1 whole, which is shorter than its diff:
```python
import functools
import math

import jax
import jax.numpy as jnp
from jax import lax
from jax.experimental import pallas as pl
from jax.experimental.pallas import tpu as pltpu
from jax.sharding import PartitionSpec as P

D = 1024
HEADS = 16
HEAD_DIM = D // HEADS
BLK = 128
SLOTS = 12
ROW = 16
QUAD = 4
OUT = BLK + 16
LOG2 = math.log2(math.e) / math.sqrt(HEAD_DIM)
LOW = -1e30


def owner_lists(block_lists, block_counts, per_device):
    first = (lax.axis_index("grid") - 1) * per_device
    ids = block_lists - first
    slot = jnp.arange(SLOTS, dtype=jnp.int32)
    live = slot[None, :] < block_counts[:, None]
    out = []
    for owner in range(3):
        here = ids - owner * per_device
        mine = live & (here >= 0) & (here < per_device)
        before = slot[:, None] < slot[None, :]
        place = jnp.sum(mine[:, :, None] & before[None], axis=1, dtype=jnp.int32)
        hit = mine[:, :, None] & (place[:, :, None] == jnp.arange(ROW)[None, None, :])
        packed = jnp.sum(jnp.where(hit, here[:, :, None], 0), axis=1)
        count = jnp.sum(mine, axis=1, dtype=jnp.int32)
        out.append(jnp.where(jnp.arange(ROW)[None, :] == SLOTS, count[:, None], packed))
    return jnp.stack(out)


def partial_kernel(make_vt, lists, q_ref, k_ref, v_ref, o_ref, *rest):
    if make_vt:
        vt, steps, s_ref, acc_ref = rest
    else:
        vt = v_ref
        steps, s_ref, acc_ref = rest
    blocks = o_ref.shape[0]
    if make_vt:

        def turn(c, carry):
            vt[c, 0:BLK, :] = v_ref[pl.ds(pl.multiple_of(c * BLK, BLK), BLK), :].T
            vt[c, BLK:OUT, :] = jnp.ones((OUT - BLK, BLK), jnp.bfloat16)
            return carry

        lax.fori_loop(0, vt.shape[0], turn, 0, unroll=4)

    def clear(b, at):
        o_ref[b] = jnp.zeros((OUT, BLK), jnp.bfloat16)
        for t in range(SLOTS // QUAD):
            steps[at + t] = b * 4 + t
        return at + (lists[b * ROW + SLOTS] + QUAD - 1) // QUAD

    steps[0] = 0
    total = lax.fori_loop(0, blocks, clear, jnp.int32(0))
    last = steps[jnp.maximum(total - 1, 0)]
    for t in range(3):
        steps[total + t] = last // 4 * 4 + 3
    acc_ref[...] = jnp.zeros_like(acc_ref)
    row128 = lax.broadcasted_iota(jnp.int32, (BLK, BLK), 0)
    row16 = lax.broadcasted_iota(jnp.int32, (OUT - BLK, BLK), 0)

    def ids_of(t):
        step = steps[t]
        b, part = step // 4, step % 4
        base = b * ROW
        count = lists[base + SLOTS]
        ids = [lists[base + jnp.minimum(part * QUAD + j, SLOTS - 1)] for j in range(QUAD)]
        dead = [part * QUAD + j >= count for j in range(QUAD)]
        return b, part, ids, dead

    def score(t, par, m_before):
        b, part, ids, dead = ids_of(t)
        qt = q_ref[pl.ds(pl.multiple_of(b * BLK, BLK), BLK), :].T
        zero = jnp.zeros_like(qt)
        q_both = jnp.concatenate(
            [jnp.where(row128 < HEAD_DIM, qt, zero), jnp.where(row128 >= HEAD_DIM, qt, zero)], axis=1
        )
        top = None
        for j in range(QUAD):
            keys = k_ref[pl.ds(pl.multiple_of(ids[j] * BLK, BLK), BLK), :]
            s = jnp.dot(keys, q_both, preferred_element_type=jnp.float32)
            s_ref[par, pl.ds(j * BLK, BLK), :] = s
            m = jnp.max(s.reshape(BLK // 8, 8, 2 * BLK), axis=0)
            m = jnp.where(dead[j], LOW, m)
            top = m if top is None else jnp.maximum(top, m)
        top = jnp.max(top, axis=0, keepdims=True) * LOG2
        top = top.astype(jnp.bfloat16).astype(jnp.float32)
        m_before = jnp.where(part == 0, LOW, m_before)
        m_now = jnp.maximum(m_before, top)
        return m_now, jnp.exp2(m_before - m_now)

    def weigh(t, par, m_now, fade):
        b, part, ids, dead = ids_of(t)
        both = None
        for j in range(0, QUAD, 2):
            w = []
            for i in (j, j + 1):
                shift = m_now + jnp.where(dead[i], -LOW, 0.0)
                w.append(
                    jnp.exp2(s_ref[par, pl.ds(i * BLK, BLK), :] * LOG2 - shift).astype(jnp.bfloat16)
                )
            vals = jnp.concatenate([vt[ids[j]], vt[ids[j + 1]]], axis=1)
            d = jnp.dot(vals, jnp.concatenate(w, axis=0), preferred_element_type=jnp.float32)
            both = d if both is None else both + d
        acc0 = acc_ref[0:HEAD_DIM] * fade[:, :BLK] + both[0:HEAD_DIM, :BLK]
        acc1 = acc_ref[HEAD_DIM:BLK] * fade[:, BLK:] + both[HEAD_DIM:BLK, BLK:]
        sum0 = acc_ref[BLK : BLK + 8] * fade[:, :BLK] + both[BLK : BLK + 8, :BLK]
        sum1 = acc_ref[BLK + 8 : OUT] * fade[:, BLK:] + both[BLK : BLK + 8, BLK:]
        acc_ref[0:HEAD_DIM] = acc0
        acc_ref[HEAD_DIM:BLK] = acc1
        acc_ref[BLK : BLK + 8] = sum0
        acc_ref[BLK + 8 : OUT] = sum1
        o_ref[b, 0:HEAD_DIM] = acc0.astype(jnp.bfloat16)
        o_ref[b, HEAD_DIM:BLK] = acc1.astype(jnp.bfloat16)
        high0 = sum0.astype(jnp.bfloat16).astype(jnp.float32)
        high1 = sum1.astype(jnp.bfloat16).astype(jnp.float32)
        stats = jnp.zeros((OUT - BLK, BLK), jnp.float32)
        for i, line in enumerate(
            (m_now[:, :BLK], high0[0:1], (sum0 - high0)[0:1], m_now[:, BLK:], high1[0:1], (sum1 - high1)[0:1])
        ):
            stats = jnp.where(row16 == i, line, stats)
        o_ref[b, BLK:OUT] = stats.astype(jnp.bfloat16)

    start = jnp.full((1, 2 * BLK), LOW, jnp.float32)
    m0, f0 = score(0, 0, start)

    def pair(i, carry):
        m0, f0 = carry
        t = 2 * i
        m1, f1 = score(t + 1, 1, m0)
        weigh(t, 0, m0, f0)
        m2, f2 = score(t + 2, 0, m1)
        weigh(t + 1, 1, m1, f1)
        return m2, f2

    lax.fori_loop(0, (total + 1) // 2, pair, (m0, f0))


def partial(lists, q, k, v, make_vt, name, blocks):
    per_device = k.shape[0] // BLK
    shapes = [jax.ShapeDtypeStruct((blocks, OUT, BLK), jnp.bfloat16)]
    if make_vt:
        shapes.append(jax.ShapeDtypeStruct((per_device, OUT, BLK), jnp.bfloat16))
    vmem = pl.BlockSpec(memory_space=pltpu.VMEM)
    return pl.pallas_call(
        functools.partial(partial_kernel, make_vt),
        out_shape=shapes,
        in_specs=[pl.BlockSpec(memory_space=pltpu.SMEM), vmem, vmem, vmem],
        out_specs=[vmem] * len(shapes),
        scratch_shapes=[
            pltpu.SMEM((blocks * 3 + 8,), jnp.int32),
            pltpu.VMEM((2, QUAD * BLK, 2 * BLK), jnp.float32),
            pltpu.VMEM((OUT, BLK), jnp.float32),
        ],
        compiler_params=pltpu.CompilerParams(vmem_limit_bytes=32 << 20),
        cost_estimate=pl.CostEstimate(flops=8_000_000_000, bytes_accessed=6 << 20, transcendentals=5_000_000),
        name=name,
    )(lists, q, k, v)


def combine_kernel(own, left, right, o_ref):
    def one(b, carry):
        parts = (own[b], left[b], right[b])
        stats = [p[BLK:OUT].astype(jnp.float32) for p in parts]
        heads = []
        for h in range(2):
            sums = [s[3 * h + 1 : 3 * h + 2] + s[3 * h + 2 : 3 * h + 3] for s in stats]
            tops = [jnp.where(l > 0, s[3 * h : 3 * h + 1], LOW) for s, l in zip(stats, sums)]
            top = jnp.maximum(jnp.maximum(tops[0], tops[1]), tops[2])
            scale = [jnp.exp2(t - top) for t in tops]
            total = sum(l * c for l, c in zip(sums, scale))
            rows = slice(h * HEAD_DIM, (h + 1) * HEAD_DIM)
            heads.append(sum(p[rows].astype(jnp.float32) * (c / total) for p, c in zip(parts, scale)))
        both = jnp.concatenate(heads, axis=0).T
        o_ref[pl.ds(pl.multiple_of(b * BLK, BLK), BLK), :] = both.astype(jnp.bfloat16)
        return carry

    lax.fori_loop(0, own.shape[0], one, 0, unroll=4)


def combine(own, left, right):
    vmem = pl.BlockSpec(memory_space=pltpu.VMEM)
    return pl.pallas_call(
        combine_kernel,
        out_shape=jax.ShapeDtypeStruct((own.shape[0] * BLK, BLK), jnp.bfloat16),
        in_specs=[vmem] * 3,
        out_specs=vmem,
        compiler_params=pltpu.CompilerParams(vmem_limit_bytes=32 << 20),
        name="combine",
    )(own, left, right)


def local(queries, resid, keys, values, w_out, block_lists, block_counts):
    blocks = queries.shape[0] // BLK
    per_device = keys.shape[0] // BLK
    lists = owner_lists(block_lists, block_counts, per_device)
    coded = lists.astype(jnp.bfloat16).reshape(-1, BLK)
    coded = jnp.pad(coded, ((0, 16 - coded.shape[0]), (0, 0)))
    packed = jnp.concatenate([queries, coded], axis=0)
    count = lax.axis_size("grid")
    up = [(i, i + 1) for i in range(count - 1)]
    down = [(i + 1, i) for i in range(count - 1)]
    from_left = lax.ppermute(packed, "grid", up)
    from_right = lax.ppermute(packed, "grid", down)
    own, vt = partial(lists[1].reshape(-1), queries, keys, values, True, "own_part", blocks)

    def lists_in(got, owner):
        rows = 3 * blocks * ROW // BLK
        got = lax.slice_in_dim(got, blocks * BLK, blocks * BLK + rows, axis=0)
        return got.astype(jnp.int32).reshape(3, -1)[owner]

    [for_left] = partial(lists_in(from_left, 2), from_left, keys, vt, False, "left_part", blocks)
    left_back = lax.ppermute(for_left, "grid", down)
    [for_right] = partial(lists_in(from_right, 0), from_right, keys, vt, False, "right_part", blocks)
    right_back = lax.ppermute(for_right, "grid", up)
    attended = combine(own, left_back, right_back)
    arrived = lax.all_to_all(attended, "head", split_axis=0, concat_axis=1, tiled=True)
    projected = jnp.dot(arrived, w_out, preferred_element_type=jnp.float32).astype(jnp.bfloat16)
    home = lax.all_to_all(projected, "head", split_axis=1, concat_axis=0, tiled=True)
    return (resid.astype(jnp.float32) + home.astype(jnp.float32)).astype(jnp.bfloat16)


def solution(mesh):
    placed = (
        P("grid", "head"),
        P("grid", "head"),
        P("grid", "head"),
        P("grid", "head"),
        P(),
        P("grid", None),
        P("grid"),
    )
    return jax.shard_map(
        local, mesh=mesh, in_specs=placed, out_specs=P("grid", "head"), check_vma=False
    )
```

time: 358 us -> 126 us (0.35)
  the two profiles are of different devices: /device:TPU:24 before, /device:TPU:4 now
where the time goes in v1:
time: 126 us
  Pallas kernels  42 us (33%)
  blocking collectives  34.4 us (27%)
  waiting for transfers between devices  21.4 us (17%)
  starting transfers between devices  14.9 us (12%)
  other arithmetic  6.87 us (5%)
  local copies, waits for them, and re-layouts  4.68 us (4%)
  matrix products  1.3 us (1%)
    pallas_call x3, Pallas kernels, partial(): pl.pallas_call(functools.partial(partial_kernel, make_vt), out_shape=shap...  40.5 us
    ppermute x1, waiting for transfers between devices, local(): right_back = lax.ppermute(for_right, 'grid', up)  19.9 us
    all_to_all x1, blocking collectives, local(): lax.all_to_all(attended, 'head', split_axis=0, concat_axis=1, tiled=True)  19.6 us
    all_to_all x1, blocking collectives, local(): lax.all_to_all(projected, 'head', split_axis=1, concat_axis=0, tiled=True)  14.7 us
    ppermute x1, starting transfers between devices, local(): left_back = lax.ppermute(for_left, 'grid', down)  5.91 us
    ppermute x1, starting transfers between devices, local(): from_right = lax.ppermute(packed, 'grid', down)  5.15 us
    unnamed x10, local copies, waits for them, and re-layouts  2.83 us
  transfers between devices with their start and end apart: 4, of which 2 were waited for; matrix products, arithmetic and copies ran while one was open for 1% of the time, Pallas kernels for 32%

profile of v1, /device:TPU:4, one launch (start us, length us, event | category | flops | bytes accessed | tf_op | source)
XLA Modules:
  0.0 125.7 jit_solution(17066127628296864679)
XLA Ops:
  0.0 0.9 convert_reduce_fusion.4
  0.9 0.7 convert_reduce_fusion.5
  1.7 0.1 convert_reduce_fusion.1
  1.8 0.1 select_reduce_fusion
  1.9 0.1 fusion.9
  2.0 0.1 copy.41
  2.1 0.1 convert_element_type.52
  2.2 2.3 %fusion.3 = bf16[4112,128]{1,0:T(8,128)(2,1)} fusion(bf16[12,128]{1,0:T(8,128)(2,1)S(1)} %convert_element_type.52, bf16[4096,128]{1,0:T(8,128)(2,1)} %q_ref.1), kind=kLoop, calls=%fused_computation.6 | loop fusion | flops 3158016 | bytes 2104320 | tf_op jit(solution)/shard_map/concatenate | solution.py:209
  4.4 1.9 %collective-permute-start = (bf16[4112,128]{1,0:T(8,128)(2,1)}, bf16[4112,128]{1,0:T(8,128)(2,1)}, u32[]{:S(2)}, u32[]{:S(2)}) collective-permute-start(bf16[4112,128]{1,0:T(8,128)(2,1)} %fusion.3), channel_id=1, source_target_pairs={{0,8},{8,16},{16,24},{24,32},{32,40},{40,48},{48,56},{56,64},{64,7... | collective-permute-start | bytes 3158024 | tf_op jit(solution)/shard_map/ppermute | solution.py:213
  6.4 5.1 %collective-permute-start.2 = (bf16[4112,128]{1,0:T(8,128)(2,1)}, bf16[4112,128]{1,0:T(8,128)(2,1)}, u32[]{:S(2)}, u32[]{:S(2)}) collective-permute-start(bf16[4112,128]{1,0:T(8,128)(2,1)} %fusion.3), channel_id=1, source_target_pairs={{8,0},{16,8},{24,16},{32,24},{40,32},{48,40},{56,48},{64,56},{72,6... | collective-permute-start | bytes 3158024 | tf_op jit(solution)/shard_map/ppermute | solution.py:214
  11.5 0.1 broadcast_select_fusion
  11.6 0.1 copy.40
  11.7 0.1 select_n.49.lists
  11.8 1.4 %copy-done.2 = bf16[6144,128]{1,0:T(8,128)(2,1)S(1)} copy-done((bf16[6144,128]{1,0:T(8,128)(2,1)S(1)}, bf16[6144,128]{1,0:T(8,128)(2,1)}, u32[]{:S(2)}) %copy-start.2) | copy-done | bytes 1572888
  13.2 1.4 %copy-done.3 = bf16[6144,128]{1,0:T(8,128)(2,1)S(1)} copy-done((bf16[6144,128]{1,0:T(8,128)(2,1)S(1)}, bf16[6144,128]{1,0:T(8,128)(2,1)}, u32[]{:S(2)}) %copy-start.3) | copy-done | bytes 1572888
  14.6 17.1 %own_part.1 = (bf16[32,144,128]{2,1,0:T(8,128)(2,1)S(1)}, bf16[48,144,128]{2,1,0:T(8,128)(2,1)S(1)}) custom-call(s32[512]{0:T(512)S(1)} %select_n.49.lists, bf16[4096,128]{1,0:T(8,128)(2,1)S(1)} %copy-done.1, bf16[6144,128]{1,0:T(8,128)(2,1)S(1)} %copy-done.3, bf16[6144,128]{1,0:T(8,128)(2,1)S(1)} %copy-done.2), custom_call_target="tpu_custom_call" | custom-call | flops 8000000000 | bytes 6291456 | tf_op jit(solution)/shard_map/own_part/pallas_call | solution.py:155
  31.7 0.7 fusion.17.lists
  32.4 11.1 %left_part.1 = bf16[32,144,128]{2,1,0:T(8,128)(2,1)S(1)} custom-call(s32[512]{0:T(512)S(1)} %fusion.17.lists, bf16[4112,128]{1,0:T(8,128)(2,1)} %collective-permute-done.q_ref, bf16[6144,128]{1,0:T(8,128)(2,1)S(1)} %copy-done.3, bf16[48,144,128]{2,1,0:T(8,128)(2,1)S(1)} %get-tuple-element.8.v_ref), custom_call_target="tpu_custom_call" | custom-call | flops 8000000000 | bytes 6291456 | tf_op jit(solution)/shard_map/left_part/pallas_call | solution.py:155
  43.5 5.9 %collective-permute-start.1 = (bf16[32,144,128]{2,1,0:T(8,128)(2,1)S(1)}, bf16[32,144,128]{2,1,0:T(8,128)(2,1)S(1)}, u32[]{:S(2)}, u32[]{:S(2)}) collective-permute-start(bf16[32,144,128]{2,1,0:T(8,128)(2,1)S(1)} %left_part.1), channel_id=1, source_target_pairs={{8,0},{16,8},{24,16},{32,24},{40,32},{48,40},{56,48},{64,56},{72,6... | collective-permute-start | bytes 3538952 | tf_op jit(solution)/shard_map/ppermute | solution.py:223
  49.5 0.7 fusion.16.lists
  50.2 12.3 %right_part.1 = bf16[32,144,128]{2,1,0:T(8,128)(2,1)S(1)} custom-call(s32[512]{0:T(512)S(1)} %fusion.16.lists, bf16[4112,128]{1,0:T(8,128)(2,1)} %collective-permute-done.2.q_ref, bf16[6144,128]{1,0:T(8,128)(2,1)S(1)} %copy-done.3, bf16[48,144,128]{2,1,0:T(8,128)(2,1)S(1)} %get-tuple-element.8.v_ref), custom_call_target="tpu_custom_call" | custom-call | flops 8000000000 | bytes 6291456 | tf_op jit(solution)/shard_map/right_part/pallas_call | solution.py:155
  62.4 1.9 %collective-permute-start.3 = (bf16[32,144,128]{2,1,0:T(8,128)(2,1)S(1)}, bf16[32,144,128]{2,1,0:T(8,128)(2,1)S(1)}, u32[]{:S(2)}, u32[]{:S(2)}) collective-permute-start(bf16[32,144,128]{2,1,0:T(8,128)(2,1)S(1)} %right_part.1), channel_id=1, source_target_pairs={{0,8},{8,16},{16,24},{24,32},{32,40},{40,48},{48,56},{56,64},{64,7... | collective-permute-start | bytes 3538952 | tf_op jit(solution)/shard_map/ppermute | solution.py:225
  64.3 1.5 %collective-permute-done.1.left = bf16[32,144,128]{2,1,0:T(8,128)(2,1)S(1)} collective-permute-done((bf16[32,144,128]{2,1,0:T(8,128)(2,1)S(1)}, bf16[32,144,128]{2,1,0:T(8,128)(2,1)S(1)}, u32[]{:S(2)}, u32[]{:S(2)}) %collective-permute-start.1) | collective-permute-done | bytes 1179680 | tf_op jit(solution)/shard_map/ppermute | solution.py:223
  65.9 19.9 %collective-permute-done.3.right = bf16[32,144,128]{2,1,0:T(8,128)(2,1)S(1)} collective-permute-done((bf16[32,144,128]{2,1,0:T(8,128)(2,1)S(1)}, bf16[32,144,128]{2,1,0:T(8,128)(2,1)S(1)}, u32[]{:S(2)}, u32[]{:S(2)}) %collective-permute-start.3) | collective-permute-done | bytes 1179680 | tf_op jit(solution)/shard_map/ppermute | solution.py:225
  85.8 1.4 %combine.1 = bf16[4096,128]{1,0:T(8,128)(2,1)S(1)} custom-call(bf16[32,144,128]{2,1,0:T(8,128)(2,1)S(1)} %get-tuple-element.7.own, bf16[32,144,128]{2,1,0:T(8,128)(2,1)S(1)} %collective-permute-done.1.left, bf16[32,144,128]{2,1,0:T(8,128)(2,1)S(1)} %collective-permute-done.3.right), custom_call_target="tpu_custom_call" | custom-call | tf_op jit(solution)/shard_map/combine/pallas_call | solution.py:193
  87.2 1.3 %copy.42 = bf16[8,512,128]{1,2,0:T(8,128)(2,1)} copy(bf16[8,512,128]{2,1,0:T(8,128)(2,1)S(1)} %bitcast.39) | data formatting | bytes 2097152 | tf_op jit(solution)/shard_map/all_to_all | solution.py:227
  88.6 19.6 %all_to_all.32 = bf16[8,512,128]{1,2,0:T(8,128)(2,1)S(1)} all-to-all(bf16[8,512,128]{1,2,0:T(8,128)(2,1)} %copy.42), channel_id=1, replica_groups=mesh['grid'=16,'head'=8] {'head'}, dimensions={0} | all-to-all | bytes 2097152 | tf_op jit(solution)/shard_map/all_to_all | solution.py:227
  108.2 1.3 %fusion.2 = bf16[64,8,8,128]{3,2,1,0:T(8,128)(2,1)S(1)} fusion(bf16[512,1024]{0,1:T(8,128)(2,1)S(1)} %bitcast.41, bf16[1024,1024]{1,0:T(8,128)(2,1)S(1)} %copy-done), kind=kOutput, calls=%fused_computation.5 | convolution fusion | flops 1074266112 | bytes 4194304 | tf_op jit(solution)/shard_map/dot_general | solution.py:228
  109.5 0.2 copy.46
  109.7 0.0 copy-start.4
  109.7 14.7 %all_to_all.33 = bf16[512,8,128]{2,0,1:T(8,128)(2,1)S(1)} all-to-all(bf16[512,8,128]{2,0,1:T(8,128)(2,1)S(1)} %bitcast.40), channel_id=1, replica_groups=mesh['grid'=16,'head'=8] {'head'}, dimensions={1} | all-to-all | bytes 2097152 | tf_op jit(solution)/shard_map/all_to_all | solution.py:229
  124.4 1.2 fusion.1
  (13 shorter events, 0.1 us)
Async XLA Ops:
  0.0 108.2 %copy-start = (bf16[1024,1024]{1,0:T(8,128)(2,1)S(1)}, bf16[1024,1024]{1,0:T(8,128)(2,1)}, u32[]{:S(2)}) copy-start(bf16[1024,1024]{1,0:T(8,128)(2,1)} %param.11) | copy-start | bytes 6291460
  0.0 11.7 %copy-start.1 = (bf16[4096,128]{1,0:T(8,128)(2,1)S(1)}, bf16[4096,128]{1,0:T(8,128)(2,1)}, u32[]{:S(2)}) copy-start(bf16[4096,128]{1,0:T(8,128)(2,1)} %q_ref.1) | copy-start | bytes 3145732
  4.4 27.3 %collective-permute-start = (bf16[4112,128]{1,0:T(8,128)(2,1)}, bf16[4112,128]{1,0:T(8,128)(2,1)}, u32[]{:S(2)}, u32[]{:S(2)}) collective-permute-start(bf16[4112,128]{1,0:T(8,128)(2,1)} %fusion.3), channel_id=1, source_target_pairs={{0,8},{8,16},{16,24},{24,32},{32,40},{40,48},{48,56},{56,64},{64,7... | collective-permute-start | bytes 3158024 | tf_op jit(solution)/shard_map/ppermute | solution.py:213
  6.4 43.1 %collective-permute-start.2 = (bf16[4112,128]{1,0:T(8,128)(2,1)}, bf16[4112,128]{1,0:T(8,128)(2,1)}, u32[]{:S(2)}, u32[]{:S(2)}) collective-permute-start(bf16[4112,128]{1,0:T(8,128)(2,1)} %fusion.3), channel_id=1, source_target_pairs={{8,0},{16,8},{24,16},{32,24},{40,32},{48,40},{56,48},{64,56},{72,6... | collective-permute-start | bytes 3158024 | tf_op jit(solution)/shard_map/ppermute | solution.py:214
  11.8 1.4 %copy-start.2 = (bf16[6144,128]{1,0:T(8,128)(2,1)S(1)}, bf16[6144,128]{1,0:T(8,128)(2,1)}, u32[]{:S(2)}) copy-start(bf16[6144,128]{1,0:T(8,128)(2,1)} %v_ref.1) | copy-start | bytes 4718596
  13.2 1.4 %copy-start.3 = (bf16[6144,128]{1,0:T(8,128)(2,1)S(1)}, bf16[6144,128]{1,0:T(8,128)(2,1)}, u32[]{:S(2)}) copy-start(bf16[6144,128]{1,0:T(8,128)(2,1)} %k_ref.5) | copy-start | bytes 4718596
  43.5 22.3 %collective-permute-start.1 = (bf16[32,144,128]{2,1,0:T(8,128)(2,1)S(1)}, bf16[32,144,128]{2,1,0:T(8,128)(2,1)S(1)}, u32[]{:S(2)}, u32[]{:S(2)}) collective-permute-start(bf16[32,144,128]{2,1,0:T(8,128)(2,1)S(1)} %left_part.1), channel_id=1, source_target_pairs={{8,0},{16,8},{24,16},{32,24},{40,32},{48,40},{56,48},{64,56},{72,6... | collective-permute-start | bytes 3538952 | tf_op jit(solution)/shard_map/ppermute | solution.py:223
  62.4 23.4 %collective-permute-start.3 = (bf16[32,144,128]{2,1,0:T(8,128)(2,1)S(1)}, bf16[32,144,128]{2,1,0:T(8,128)(2,1)S(1)}, u32[]{:S(2)}, u32[]{:S(2)}) collective-permute-start(bf16[32,144,128]{2,1,0:T(8,128)(2,1)S(1)} %right_part.1), channel_id=1, source_target_pairs={{0,8},{8,16},{16,24},{24,32},{32,40},{40,48},{48,56},{56,64},{64,7... | collective-permute-start | bytes 3538952 | tf_op jit(solution)/shard_map/ppermute | solution.py:225
  109.7 14.7 %copy-start.4 = (bf16[4096,128]{1,0:T(8,128)(2,1)S(1)}, bf16[4096,128]{1,0:T(8,128)(2,1)}, u32[]{:S(2)}) copy-start(bf16[4096,128]{1,0:T(8,128)(2,1)} %param.8) | copy-start | bytes 3145732

commit v2 on v0

v2 whole, which is shorter than its diff:
```python
import functools
import math

import jax
import jax.numpy as jnp
from jax import lax
from jax.experimental import pallas as pl
from jax.experimental.pallas import tpu as pltpu
from jax.sharding import PartitionSpec as P

D = 1024
HEADS = 16
HEAD_DIM = D // HEADS
BLK = 128
SLOTS = 12
ROW = 16
QUAD = 4
OUT = BLK + 16
LOG2 = math.log2(math.e) / math.sqrt(HEAD_DIM)
LOW = -1e30
SUBS = 2
BF16, F32, I32 = jnp.bfloat16, jnp.float32, jnp.int32
MESH = pl.DeviceIdType.MESH


def rows(b, size=BLK):
    return pl.ds(pl.multiple_of(b * size, size), size)


def entry(lists, b, j):
    return lists[b // (BLK // ROW), b % (BLK // ROW) * ROW + j]


def place():
    count = lax.axis_size("grid")
    g = lax.axis_index("grid")
    core = lax.rem(g, 2)
    return g, core, g + 1 - 2 * core, lax.rem(g - 1 + 2 * core + count, count)


def both_heads(q):
    qt = q.T
    row = lax.broadcasted_iota(I32, (BLK, BLK), 0)
    zero = jnp.zeros_like(qt)
    return jnp.concatenate([jnp.where(row < HEAD_DIM, qt, zero), jnp.where(row >= HEAD_DIM, qt, zero)], axis=1)


def score_slots(q, k_ref, s_ref, par, ids, bias):
    q_both = both_heads(q)
    top = None
    for j, (c, less) in enumerate(zip(ids, bias)):
        s = jnp.dot(k_ref[c], q_both, preferred_element_type=F32)
        s_ref[par, pl.ds(j * BLK, BLK), :] = s
        m = jnp.max(s.reshape(BLK // 8, 8, 2 * BLK), axis=0)
        m = m - less
        top = m if top is None else jnp.maximum(top, m)
    top = jnp.max(top, axis=0, keepdims=True) * LOG2
    return top.astype(BF16).astype(F32)


def weigh_slots(s_ref, par, vt, ids, bias, top):
    both = None
    for j in range(0, len(ids), 2):
        w = []
        for i in (j, j + 1):
            shift = top + bias[i]
            w.append(jnp.exp2(s_ref[par, pl.ds(i * BLK, BLK), :] * LOG2 - shift).astype(BF16))
        vals = jnp.concatenate([vt[ids[j]], vt[ids[j + 1]]], axis=1)
        d = jnp.dot(vals, jnp.concatenate(w, axis=0), preferred_element_type=F32)
        both = d if both is None else both + d
    return both


def put_result(o_ref, b, acc0, acc1, top, sum0, sum1):
    o_ref[b, 0:HEAD_DIM] = acc0.astype(BF16)
    o_ref[b, HEAD_DIM:BLK] = acc1.astype(BF16)
    row = lax.broadcasted_iota(I32, (OUT - BLK, BLK), 0)
    high0 = sum0.astype(BF16).astype(F32)
    high1 = sum1.astype(BF16).astype(F32)
    stats = jnp.zeros((OUT - BLK, BLK), F32)
    lines = (top[:, :BLK], high0[0:1], (sum0 - high0)[0:1], top[:, BLK:], high1[0:1], (sum1 - high1)[0:1])
    for i, line in enumerate(lines):
        stats = jnp.where(row == i, line, stats)
    o_ref[b, BLK:OUT] = stats.astype(BF16)


def turn_values(v_ref, vt, first, count):
    def turn(i, carry):
        c = first + i
        vt[c, 0:BLK, :] = v_ref[c].T
        vt[c, BLK:OUT, :] = jnp.ones((OUT - BLK, BLK), BF16)
        return carry

    lax.fori_loop(0, count, turn, 0, unroll=4)


def chip_kernel(
    ids_s, bias_s, lists_h, q_h, k_h, v_h, o_ref, vt_o, qx_o, lx_o, q_ref, k_all, v_all, vt, s_ref, local_sem, send_sem, recv_sem
):
    blocks = o_ref.shape[0]
    per_device = vt_o.shape[0]
    head = lax.axis_index("head")
    g, core, mate, cross = place()
    barrier = pltpu.get_barrier_semaphore()
    for other in (mate, cross):
        pl.semaphore_signal(barrier, inc=1, device_id=(other, head), device_id_type=MESH)
    pl.semaphore_wait(barrier, 2)

    mine = pl.ds(core * per_device, per_device)

    def remote(i, src, dst, other):
        return pltpu.make_async_remote_copy(
            src_ref=src, dst_ref=dst, send_sem=send_sem.at[i], recv_sem=recv_sem.at[i],
            device_id=(other, head), device_id_type=MESH,
        )

    out_v = remote(0, v_h, v_all.at[mine], mate)
    out_k = remote(1, k_h, k_all.at[mine], mate)
    out_q = remote(2, q_h, qx_o, cross)
    out_l = remote(3, lists_h, lx_o, cross)
    in_v = pltpu.make_async_copy(v_h, v_all.at[mine], local_sem.at[0])
    in_k = pltpu.make_async_copy(k_h, k_all.at[mine], local_sem.at[1])
    in_q = pltpu.make_async_copy(q_h, q_ref, local_sem.at[2])
    for copy in (out_v, in_v, out_q, out_k, in_k, in_q, out_l):
        copy.start()
    in_v.wait()
    turn_values(v_all, vt, core * per_device, per_device)
    keep_vt = pltpu.make_async_copy(vt.at[pl.ds(core * per_device, per_device)], vt_o, local_sem.at[3])
    keep_vt.start()
    out_v.wait_recv()
    turn_values(v_all, vt, (1 - core) * per_device, per_device)
    in_k.wait()
    in_q.wait()
    out_k.wait_recv()

    def ids_of(b):
        return [entry(ids_s, b, j) for j in range(SLOTS)], [entry(bias_s, b, j) for j in range(SLOTS)]

    def score(b, par):
        ids, bias = ids_of(b)
        return score_slots(q_ref[rows(b), :], k_all, s_ref, par, ids, bias)

    def weigh(b, par, top):
        ids, bias = ids_of(b)
        both = weigh_slots(s_ref, par, vt, ids, bias, top)
        sums = both[BLK : BLK + 8]
        put_result(o_ref, b, both[0:HEAD_DIM, :BLK], both[HEAD_DIM:BLK, BLK:], top, sums[:, :BLK], sums[:, BLK:])

    def pair(i, m0):
        b = 2 * i
        m1 = score(b + 1, 1)
        weigh(b, 0, m0)
        m2 = score(jnp.minimum(b + 2, blocks - 1), 0)
        weigh(b + 1, 1, m1)
        return m2

    lax.fori_loop(0, blocks // 2, pair, score(0, 0))
    keep_vt.wait()
    out_v.wait_send()
    out_k.wait_send()
    out_q.wait()
    out_l.wait()


def chip_part(ids, bias, lists, q, k, v):
    blocks, per_device = q.shape[0] // BLK, k.shape[0]
    vmem = pl.BlockSpec(memory_space=pltpu.VMEM)
    any_ = pl.BlockSpec(memory_space=pl.ANY)
    return pl.pallas_call(
        chip_kernel,
        out_shape=[
            jax.ShapeDtypeStruct((blocks, OUT, BLK), BF16),
            jax.ShapeDtypeStruct((per_device, OUT, BLK), BF16),
            jax.ShapeDtypeStruct(q.shape, BF16),
            jax.ShapeDtypeStruct(lists.shape, I32),
        ],
        in_specs=[pl.BlockSpec(memory_space=pltpu.SMEM)] * 2 + [any_] * 4,
        out_specs=[vmem, any_, any_, any_],
        scratch_shapes=[
            pltpu.VMEM(q.shape, BF16),
            pltpu.VMEM((2 * per_device, BLK, BLK), BF16),
            pltpu.VMEM((2 * per_device, BLK, BLK), BF16),
            pltpu.VMEM((2 * per_device, OUT, BLK), BF16),
            pltpu.VMEM((2, SLOTS * BLK, 2 * BLK), F32),
            pltpu.SemaphoreType.DMA((4,)),
            pltpu.SemaphoreType.DMA((4,)),
            pltpu.SemaphoreType.DMA((4,)),
        ],
        compiler_params=pltpu.CompilerParams(vmem_limit_bytes=40 << 20, collective_id=0, has_side_effects=True),
        cost_estimate=pl.CostEstimate(flops=8_000_000_000, bytes_accessed=12 << 20, transcendentals=12_000_000),
        name="chip_part",
    )(ids, bias, lists, q, k, v)


def cross_kernel(lists, q_h, k_h, vt_h, o_ref, q_ref, k_ref, vt, found, steps, s_ref, acc_ref, sem):
    loads = [
        pltpu.make_async_copy(src, dst, sem.at[i])
        for i, (src, dst) in enumerate(((q_h, q_ref), (k_h, k_ref), (vt_h, vt)))
    ]
    for load in loads:
        load.start()
    blocks = o_ref.shape[0]
    per_device = vt.shape[0]
    low = lax.axis_index("grid") * per_device

    def search(b, at):
        count = entry(lists, b, SLOTS)
        n = jnp.int32(0)
        for j in range(SLOTS):
            c = entry(lists, b, j) - low
            found[b * ROW + n] = c
            hit = (c >= 0) & (c < per_device) & (j < count)
            n = n + hit.astype(I32)
        for j in range(QUAD - 1):
            found[b * ROW + n + j] = 0
        found[b * ROW + ROW - 1] = n
        for t in range(SLOTS // QUAD):
            steps[at + t] = b * 4 + t
        o_ref[b] = jnp.zeros((OUT, BLK), BF16)
        return at + (n + QUAD - 1) // QUAD

    steps[0] = 0
    total = lax.fori_loop(0, blocks, search, jnp.int32(0))
    last = steps[jnp.maximum(total - 1, 0)]
    for t in range(5):
        steps[total + t] = last // 4 * 4 + 3
    acc_ref[...] = jnp.zeros_like(acc_ref)
    for load in loads:
        load.wait()

    def ids_of(t):
        b, part = steps[t] // 4, steps[t] % 4
        count = found[b * ROW + ROW - 1]
        dead = [part * QUAD + j >= count for j in range(QUAD)]
        ids = [jnp.where(gone, 0, found[b * ROW + part * QUAD + j]) for j, gone in enumerate(dead)]
        return b, part, ids, [jnp.where(gone, -LOW, 0.0) for gone in dead]

    def score(t, par, before):
        b, part, ids, bias = ids_of(t)
        top = score_slots(q_ref[rows(b), :], k_ref, s_ref, par, ids, bias)
        before = jnp.where(part == 0, LOW, before)
        top = jnp.maximum(before, top)
        return top, jnp.exp2(before - top)

    def weigh(t, par, top, fade):
        b, part, ids, bias = ids_of(t)
        both = weigh_slots(s_ref, par, vt, ids, bias, top)
        acc0 = acc_ref[0:HEAD_DIM] * fade[:, :BLK] + both[0:HEAD_DIM, :BLK]
        acc1 = acc_ref[HEAD_DIM:BLK] * fade[:, BLK:] + both[HEAD_DIM:BLK, BLK:]
        sum0 = acc_ref[BLK : BLK + 8] * fade[:, :BLK] + both[BLK : BLK + 8, :BLK]
        sum1 = acc_ref[BLK + 8 : OUT] * fade[:, BLK:] + both[BLK : BLK + 8, BLK:]
        acc_ref[0:HEAD_DIM] = acc0
        acc_ref[HEAD_DIM:BLK] = acc1
        acc_ref[BLK : BLK + 8] = sum0
        acc_ref[BLK + 8 : OUT] = sum1
        put_result(o_ref, b, acc0, acc1, top, sum0, sum1)

    def four(i, carry):
        now = carry
        for j in range(4):
            t = 4 * i + j
            then = score(t + 1, (j + 1) % 4, now[0])
            weigh(t, j, *now)
            now = then
        return now

    start = jnp.full((1, 2 * BLK), LOW, F32)
    lax.fori_loop(0, (total + 3) // 4, four, score(0, 0, start))


def cross_part(lists, q, k, vt):
    blocks = q.shape[0] // BLK
    any_ = pl.BlockSpec(memory_space=pl.ANY)
    return pl.pallas_call(
        cross_kernel,
        out_shape=jax.ShapeDtypeStruct((blocks, OUT, BLK), BF16),
        in_specs=[pl.BlockSpec(memory_space=pltpu.SMEM), any_, any_, any_],
        out_specs=pl.BlockSpec(memory_space=pltpu.VMEM),
        scratch_shapes=[
            pltpu.VMEM(q.shape, BF16),
            pltpu.VMEM(k.shape, BF16),
            pltpu.VMEM(vt.shape, BF16),
            pltpu.SMEM((blocks * ROW,), I32),
            pltpu.SMEM((blocks * 3 + 8,), I32),
            pltpu.VMEM((4, QUAD * BLK, 2 * BLK), F32),
            pltpu.VMEM((OUT, BLK), F32),
            pltpu.SemaphoreType.DMA((3,)),
        ],
        compiler_params=pltpu.CompilerParams(vmem_limit_bytes=32 << 20),
        name="cross_part",
    )(lists, q, k, vt)


def combine(parts):
    stats = [p[BLK:OUT].astype(F32) for p in parts]
    heads = []
    for h in range(2):
        sums = [s[3 * h + 1 : 3 * h + 2] + s[3 * h + 2 : 3 * h + 3] for s in stats]
        tops = [jnp.where(l > 0, s[3 * h : 3 * h + 1], LOW) for s, l in zip(stats, sums)]
        top = functools.reduce(jnp.maximum, tops)
        scale = [jnp.exp2(t - top) for t in tops]
        total = sum(l * c for l, c in zip(sums, scale))
        part = slice(h * HEAD_DIM, (h + 1) * HEAD_DIM)
        heads.append(sum(p[part].astype(F32) * (c / total) for p, c in zip(parts, scale)))
    return jnp.concatenate(heads, axis=0).T.astype(BF16)


def project_kernel(own, other, w_h, home, got, att, w_ref, stage, w_sem, own_sem, send_sem, recv_sem, back_sem, home_sem):
    heads = lax.axis_size("head")
    head = lax.axis_index("head")
    g, core, mate, cross = place()
    blocks = own.shape[0] // heads
    per_sub = blocks // SUBS
    load_w = pltpu.make_async_copy(w_h, w_ref, w_sem)
    load_w.start()
    barrier = pltpu.get_barrier_semaphore()
    for i in range(1, heads):
        pl.semaphore_signal(barrier, inc=1, device_id=(g, lax.rem(head + i, heads)), device_id_type=MESH)
    for i in range(heads):
        pl.semaphore_signal(barrier, inc=1, device_id=(cross, lax.rem(head + i, heads)), device_id_type=MESH)
    pl.semaphore_wait(barrier, 2 * heads - 1)

    def to_own(s, i):
        to = lax.rem(head + i, heads)
        return pltpu.make_async_remote_copy(
            src_ref=own.at[pl.ds(to * blocks + s * per_sub, per_sub)],
            dst_ref=got.at[0, i, pl.ds(s * per_sub, per_sub)],
            send_sem=send_sem.at[0, s, i], recv_sem=recv_sem.at[0, s, i],
            device_id=(g, to), device_id_type=MESH,
        )

    def to_cross(s, i):
        to = lax.rem(head + i, heads)
        return pltpu.make_async_remote_copy(
            src_ref=other.at[pl.ds(to * blocks + s * per_sub, per_sub)],
            dst_ref=got.at[1, i, pl.ds(s * per_sub, per_sub)],
            send_sem=send_sem.at[1, s, i], recv_sem=recv_sem.at[1, s, i],
            device_id=(cross, to), device_id_type=MESH,
        )

    keep = pltpu.make_async_copy(own.at[pl.ds(head * blocks, blocks)], got.at[0, 0], own_sem)
    keep.start()
    for s in range(SUBS):
        for i in range(heads):
            to_cross(s, i).start()
            if i:
                to_own(s, i).start()
    keep.wait()
    load_w.wait()

    def back(s, i):
        to = lax.rem(head + i, heads)
        return pltpu.make_async_remote_copy(
            src_ref=stage.at[to, pl.ds(s * per_sub * BLK, per_sub * BLK)],
            dst_ref=home.at[pl.ds(pl.multiple_of(head * blocks * BLK, BLK) + s * per_sub * BLK, per_sub * BLK)],
            send_sem=back_sem.at[s, i], recv_sem=home_sem.at[s, i],
            device_id=(g, to), device_id_type=MESH,
        )

    for s in range(SUBS):
        for i in range(heads):
            to_cross(s, i).wait_recv()
            if i:
                to_own(s, i).wait_recv()
            source = lax.rem(head - i + heads, heads)
            for n in range(per_sub):
                b = s * per_sub + n
                att[pl.ds(b * BLK, BLK), rows(source)] = combine((got[0, i, b], got[1, i, b]))
        size = per_sub * BLK
        for n in range(0, D, 256):
            out = jnp.dot(att[pl.ds(s * size, size), :], w_ref[:, n : n + 256], preferred_element_type=F32).astype(BF16)
            for c in range(2):
                stage[n // BLK + c, pl.ds(s * size, size), :] = out[:, c * BLK : (c + 1) * BLK]
        for i in range(1, heads):
            back(s, i).start()
        home[pl.ds(pl.multiple_of(head * blocks * BLK, BLK) + s * size, size), :] = stage[head, pl.ds(s * size, size), :]
    for s in range(SUBS):
        for i in range(heads):
            to_cross(s, i).wait_send()
            if i:
                to_own(s, i).wait_send()
                back(s, i).wait()


def project(own, other, w_out):
    heads = lax.axis_size("head")
    blocks = own.shape[0] // heads
    vmem = pl.BlockSpec(memory_space=pltpu.VMEM)
    return pl.pallas_call(
        project_kernel,
        out_shape=jax.ShapeDtypeStruct((own.shape[0] * BLK, BLK), BF16),
        in_specs=[vmem, vmem, pl.BlockSpec(memory_space=pl.ANY)],
        out_specs=vmem,
        scratch_shapes=[
            pltpu.VMEM((2, heads, blocks, OUT, BLK), BF16),
            pltpu.VMEM((blocks * BLK, D), BF16),
            pltpu.VMEM((D, D), BF16),
            pltpu.VMEM((heads, blocks * BLK, BLK), BF16),
            pltpu.SemaphoreType.DMA,
            pltpu.SemaphoreType.DMA,
            pltpu.SemaphoreType.DMA((2, SUBS, heads)),
            pltpu.SemaphoreType.DMA((2, SUBS, heads)),
            pltpu.SemaphoreType.DMA((SUBS, heads)),
            pltpu.SemaphoreType.DMA((SUBS, heads)),
        ],
        compiler_params=pltpu.CompilerParams(vmem_limit_bytes=32 << 20, collective_id=1, has_side_effects=True),
        name="project",
    )(own, other, w_out)


def local(queries, resid, keys, values, w_out, block_lists, block_counts):
    per_device = keys.shape[0] // BLK
    keys, values = keys.reshape(-1, BLK, BLK), values.reshape(-1, BLK, BLK)

    def table(a):
        return jnp.pad(a, ((0, 8 * BLK // ROW - a.shape[0]), (0, ROW - a.shape[1]))).reshape(8, BLK)

    g = lax.axis_index("grid")
    near = block_lists - (g - lax.rem(g, 2)) * per_device
    used = jnp.arange(SLOTS, dtype=jnp.int32)[None, :] < block_counts[:, None]
    used &= (near >= 0) & (near < 2 * per_device)
    ids, bias = table(jnp.where(used, near, 0)), table(jnp.where(used, 0.0, -LOW).astype(jnp.float32))
    lists = table(jnp.concatenate([block_lists, block_counts[:, None]], axis=1))
    own, vt, cross_q, cross_lists = chip_part(ids, bias, lists, queries, keys, values)
    other = cross_part(cross_lists, cross_q, keys, vt)
    home = project(own, other, w_out)
    return (resid.astype(jnp.float32) + home.astype(jnp.float32)).astype(jnp.bfloat16)


def solution(mesh):
    placed = (
        P("grid", "head"),
        P("grid", "head"),
        P("grid", "head"),
        P("grid", "head"),
        P(),
        P("grid", None),
        P("grid"),
    )
    return jax.shard_map(
        local, mesh=mesh, in_specs=placed, out_specs=P("grid", "head"), check_vma=False
    )
```

time: 358 us -> 95.8 us (0.27); the launches traced: 353 us -> 95.5 us
  local copies, waits for them, and re-layouts: 179 us -> 4.56 us
  Pallas kernels: 0 us -> 87.5 us
  waiting for transfers between devices: 67.5 us -> 0 us
  matrix products: 36.3 us -> 0 us
  blocking collectives: 31.7 us -> 0 us
  other arithmetic: 26.8 us -> 3.37 us
  starting transfers between devices: 11.8 us -> 0 us
    squeeze x8 -> x0, local copies, waits for them, and re-layouts: 93.4 us -> none  [one_group(): block_k = tiles[0][block_ids].reshape(group, slots * BLK, width)]
    pallas_call x0 -> x3, Pallas kernels: none -> 87.5 us  [the longest x1 49.6 us: project(): pl.pallas_call(project_kernel, out_shape=jax.ShapeDtypeStruct((own.shape[...]
    gather x16 -> x0, local copies, waits for them, and re-layouts: 68.7 us -> none  [the longest x8 34.4 us: one_group(): block_v = tiles[1][block_ids].reshape(group, slots * BLK, width)]
    ppermute x2 -> x0, waiting for transfers between devices: 67.5 us -> none  [the longest x1 59.4 us: extended(): lax.ppermute(head, axis, [((i + 1) % count, i) for i in range(ends)])]
    dot_general x17 -> x0, matrix products: 36.3 us -> none  [the longest x8 19.9 us: one_group(): jnp.einsum('ghqc,gkc->ghqk', masked_q, block_k, preferred_element_type=jn...]
    all_to_all x2 -> x0, blocking collectives: 31.7 us -> none  [the longest x1 17.6 us: local(): lax.all_to_all(attended, 'head', split_axis=0, concat_axis=1, tiled=True)]
    reduce_sum x8 -> x0, other arithmetic: 11 us -> none  [one_group(): total = jnp.sum(weight, axis=-1, keepdims=True)]
    concatenate x1, other arithmetic: 11.6 us -> 0.72 us  [local(): lists = table(jnp.concatenate([block_lists, block_counts[:, None]], axis=1))]
  transfers between devices with their start and end apart: 3 -> 0, of which waited for: 2 -> 0; matrix products, arithmetic and copies ran while one was open for 67% -> 0% of each run, Pallas kernels for 0% -> 0%
where the time goes in v2:
time: 95.8 us; the launch traced here: 95.5 us
  Pallas kernels  87.5 us (91%)
  local copies, waits for them, and re-layouts  4.56 us (5%)
  other arithmetic  3.37 us (4%)
    pallas_call x1, Pallas kernels, project(): pl.pallas_call(project_kernel, out_shape=jax.ShapeDtypeStruct((own.shape[...  49.6 us
    pallas_call x1, Pallas kernels, chip_part(): pl.pallas_call(chip_kernel, out_shape=[jax.ShapeDtypeStruct((blocks, OUT,...  28.2 us
    pallas_call x1, Pallas kernels, cross_part(): pl.pallas_call(cross_kernel, out_shape=jax.ShapeDtypeStruct((blocks, OUT,...  9.61 us
    unnamed x13, local copies, waits for them, and re-layouts  4.31 us

profile of v2, /device:TPU:24, one launch (start us, length us, event | category | flops | bytes accessed | tf_op | source)
XLA Modules:
  0.0 95.5 jit_solution(9074027398386744231)
XLA Ops:
  0.0 0.7 pad_add_fusion
  0.7 0.1 copy.16
  0.8 0.7 broadcast_select_fusion
  1.5 0.7 subtract_select_fusion
  2.2 0.1 copy.14
  2.3 0.1 copy.15
  2.4 0.1 reshape.17.bias_s
  2.5 0.1 reshape.16.ids_s
  2.6 0.1 reshape.18.lists_h
  2.7 0.0 copy-start.1
  2.7 1.4 %copy-done.1 = bf16[6144,128]{1,0:T(8,128)(2,1)S(1)} copy-done((bf16[6144,128]{1,0:T(8,128)(2,1)S(1)}, bf16[6144,128]{1,0:T(8,128)(2,1)}, u32[]{:S(2)}) %copy-start.1) | copy-done | bytes 1572888
  4.1 0.0 copy-start.2
  4.1 1.4 %copy-done.2 = bf16[6144,128]{1,0:T(8,128)(2,1)S(1)} copy-done((bf16[6144,128]{1,0:T(8,128)(2,1)S(1)}, bf16[6144,128]{1,0:T(8,128)(2,1)}, u32[]{:S(2)}) %copy-start.2) | copy-done | bytes 1572888
  5.5 0.0 copy-start.3
  5.5 1.2 %copy-done.3 = bf16[4096,128]{1,0:T(8,128)(2,1)S(1)} copy-done((bf16[4096,128]{1,0:T(8,128)(2,1)S(1)}, bf16[4096,128]{1,0:T(8,128)(2,1)}, u32[]{:S(2)}) %copy-start.3) | copy-done | bytes 1048600
  6.7 28.2 %chip_part.1 = (bf16[32,144,128]{2,1,0:T(8,128)(2,1)S(1)}, bf16[48,144,128]{2,1,0:T(8,128)(2,1)S(1)}, bf16[4096,128]{1,0:T(8,128)(2,1)S(1)}, s32[8,128]{1,0:T(8,128)S(1)}) custom-call(s32[8,128]{1,0:T(8,128)S(1)} %reshape.16.ids_s, f32[8,128]{1,0:T(8,128)S(1)} %reshape.17.bias_s, s32[8,128]{1,0:T(8,128)S(1)} %reshape.18.lists_h, ...), custom_call_target="tpu_custom_call" | custom-call | flops 8000000000 | bytes 12582912 | tf_op jit(solution)/shard_map/chip_part/pallas_call | solution.py:169
  34.9 0.0 copy-start
  34.9 9.6 %cross_part.1.other = bf16[32,144,128]{2,1,0:T(8,128)(2,1)S(1)} custom-call(s32[8,128]{1,0:T(8,128)S(1)} %get-tuple-element.10.lists, bf16[4096,128]{1,0:T(8,128)(2,1)S(1)} %get-tuple-element.11.q_h, bf16[48,128,128]{2,1,0:T(8,128)(2,1)S(1)} %bitcast.4, bf16[48,144,128]{2,1,0:T(8,128)(2,1)S(1)} %get-tuple-element.12.vt_h), custom_call_target="tpu_custom_call" | custom-call | tf_op jit(solution)/shard_map/cross_part/pallas_call | solution.py:274
  44.5 0.0 copy-done
  44.6 0.0 copy-start.4
  44.6 49.6 %project.1 = bf16[4096,128]{1,0:T(8,128)(2,1)S(1)} custom-call(bf16[32,144,128]{2,1,0:T(8,128)(2,1)S(1)} %get-tuple-element.9.own, bf16[32,144,128]{2,1,0:T(8,128)(2,1)S(1)} %cross_part.1.other, bf16[1024,1024]{1,0:T(8,128)(2,1)S(1)} %copy-done), custom_call_target="tpu_custom_call" | custom-call | tf_op jit(solution)/shard_map/project/pallas_call | solution.py:389
  94.2 0.0 copy-done.4
  94.2 1.2 %add_convert_fusion = bf16[4096,128]{1,0:T(8,128)(2,1)} fusion(bf16[4096,128]{1,0:T(8,128)(2,1)S(1)} %project.1, bf16[4096,128]{1,0:T(8,128)(2,1)S(1)} %copy-done.4), kind=kLoop, calls=%fused_computation | loop fusion | flops 2097152 | bytes 3145728 | tf_op jit(solution)/shard_map/convert_element_type | solution.py:427
  (3 shorter events, 0.0 us)
Async XLA Ops:
  2.7 1.4 %copy-start.1 = (bf16[6144,128]{1,0:T(8,128)(2,1)S(1)}, bf16[6144,128]{1,0:T(8,128)(2,1)}, u32[]{:S(2)}) copy-start(bf16[6144,128]{1,0:T(8,128)(2,1)} %param.9) | copy-start | bytes 4718596
  4.1 1.4 %copy-start.2 = (bf16[6144,128]{1,0:T(8,128)(2,1)S(1)}, bf16[6144,128]{1,0:T(8,128)(2,1)}, u32[]{:S(2)}) copy-start(bf16[6144,128]{1,0:T(8,128)(2,1)} %param.10) | copy-start | bytes 4718596
  5.5 1.2 %copy-start.3 = (bf16[4096,128]{1,0:T(8,128)(2,1)S(1)}, bf16[4096,128]{1,0:T(8,128)(2,1)}, u32[]{:S(2)}) copy-start(bf16[4096,128]{1,0:T(8,128)(2,1)} %q_h.1) | copy-start | bytes 3145732
  34.9 9.6 %copy-start = (bf16[1024,1024]{1,0:T(8,128)(2,1)S(1)}, bf16[1024,1024]{1,0:T(8,128)(2,1)}, u32[]{:S(2)}) copy-start(bf16[1024,1024]{1,0:T(8,128)(2,1)} %w_h.1) | copy-start | bytes 6291460
  44.6 49.7 %copy-start.4 = (bf16[4096,128]{1,0:T(8,128)(2,1)S(1)}, bf16[4096,128]{1,0:T(8,128)(2,1)}, u32[]{:S(2)}) copy-start(bf16[4096,128]{1,0:T(8,128)(2,1)} %param.8) | copy-start | bytes 3145732

commit v3 on v0

v3 whole, which is shorter than its diff:
```python
import functools
import math

import jax
import jax.numpy as jnp
from jax import lax
from jax.experimental import pallas as pl
from jax.experimental.pallas import tpu as pltpu
from jax.sharding import PartitionSpec as P

D = 1024
HEADS = 16
HEAD_DIM = D // HEADS
BLK = 128
SLOTS = 12
ROW = 16
OUT = BLK + 16
LOG2 = math.log2(math.e) / math.sqrt(HEAD_DIM)
LOW = -1e30
SUBLINES = 4
SUBS = 2
BF16, F32, I32 = jnp.bfloat16, jnp.float32, jnp.int32
MESH = pl.DeviceIdType.MESH


def rows(b, size=BLK):
    return pl.ds(pl.multiple_of(b * size, size), size)


def place():
    count = lax.axis_size("grid")
    g = lax.axis_index("grid")
    core = lax.rem(g, 2)
    return g, core, g + 1 - 2 * core, lax.rem(g - 1 + 2 * core + count, count)


def both_heads(q):
    qt = q.T
    row = lax.broadcasted_iota(I32, (BLK, BLK), 0)
    zero = jnp.zeros_like(qt)
    return jnp.concatenate([jnp.where(row < HEAD_DIM, qt, zero), jnp.where(row >= HEAD_DIM, qt, zero)], axis=1)


def score_slots(q, k_ref, s_ref, par, ids, bias):
    q_both = both_heads(q)
    top = None
    for j, (c, less) in enumerate(zip(ids, bias)):
        s = jnp.dot(k_ref[c], q_both, preferred_element_type=F32)
        s_ref[par, pl.ds(j * BLK, BLK), :] = s
        m = jnp.max(s.reshape(BLK // 8, 8, 2 * BLK), axis=0)
        m = m - less
        top = m if top is None else jnp.maximum(top, m)
    top = jnp.max(top, axis=0, keepdims=True) * LOG2
    return top.astype(BF16).astype(F32)


def weigh_slots(s_ref, par, vt, ids, bias, top):
    both = None
    for j in range(0, len(ids), 2):
        w = []
        for i in (j, j + 1):
            shift = top + bias[i]
            w.append(jnp.exp2(s_ref[par, pl.ds(i * BLK, BLK), :] * LOG2 - shift).astype(BF16))
        vals = jnp.concatenate([vt[ids[j]], vt[ids[j + 1]]], axis=1)
        d = jnp.dot(vals, jnp.concatenate(w, axis=0), preferred_element_type=F32)
        both = d if both is None else both + d
    return both


def put_result(o_ref, b, acc0, acc1, top, sum0, sum1):
    o_ref[b, 0:HEAD_DIM] = acc0.astype(BF16)
    o_ref[b, HEAD_DIM:BLK] = acc1.astype(BF16)
    row = lax.broadcasted_iota(I32, (OUT - BLK, BLK), 0)
    high0 = sum0.astype(BF16).astype(F32)
    high1 = sum1.astype(BF16).astype(F32)
    stats = jnp.zeros((OUT - BLK, BLK), F32)
    lines = (top[:, :BLK], high0[0:1], (sum0 - high0)[0:1], top[:, BLK:], high1[0:1], (sum1 - high1)[0:1])
    for i, line in enumerate(lines):
        stats = jnp.where(row == i, line, stats)
    o_ref[b, BLK:OUT] = stats.astype(BF16)


def turn_values(v_ref, vt, first, count):
    def turn(i, carry):
        c = first + i
        vt[c, 0:BLK, :] = v_ref[c].T
        vt[c, BLK:OUT, :] = jnp.ones((OUT - BLK, BLK), BF16)
        return carry

    lax.fori_loop(0, count, turn, 0, unroll=4)


def combine(parts):
    stats = [p[BLK:OUT].astype(F32) for p in parts]
    heads = []
    for h in range(2):
        sums = [s[3 * h + 1 : 3 * h + 2] + s[3 * h + 2 : 3 * h + 3] for s in stats]
        tops = [jnp.where(l > 0, s[3 * h : 3 * h + 1], LOW) for s, l in zip(stats, sums)]
        top = functools.reduce(jnp.maximum, tops)
        scale = [jnp.exp2(t - top) for t in tops]
        total = sum(l * c for l, c in zip(sums, scale))
        part = slice(h * HEAD_DIM, (h + 1) * HEAD_DIM)
        heads.append(sum(p[part].astype(F32) * (c / total) for p, c in zip(parts, scale)))
    return jnp.concatenate(heads, axis=0).T.astype(BF16)


def mixed_kernel(
    tables, q_h, k_h, v_h, w_h, home, lists_o,
    tab, q_all, k_all, v_all, vt, s_ref, done, got, att, w_ref, stage,
    tab_sem, load_sem, pair_send, pair_recv, q_send, q_recv, part_send, part_recv, back_send, back_recv,
):
    heads = lax.axis_size("head")
    head = lax.axis_index("head")
    g, core, mate, cross = place()
    per_device = k_h.shape[0]
    blocks = q_h.shape[0] // BLK // heads
    load_w = pltpu.make_async_copy(w_h, w_ref, load_sem.at[0])
    mine = pl.ds(core * per_device, per_device)
    in_v = pltpu.make_async_copy(v_h, v_all.at[mine], load_sem.at[1])
    in_k = pltpu.make_async_copy(k_h, k_all.at[mine], load_sem.at[2])
    in_q = pltpu.make_async_copy(q_h, q_all.at[0], load_sem.at[3])
    in_t = pltpu.make_async_copy(tables.at[0], tab.at[0], tab_sem.at[0])
    for load in (in_v, in_t, in_q, in_k, load_w):
        load.start()

    barrier = pltpu.get_barrier_semaphore()
    pl.semaphore_signal(barrier, inc=1, device_id=(mate, head), device_id_type=MESH)
    for i in range(heads):
        to = lax.rem(head + i, heads)
        pl.semaphore_signal(barrier, inc=1, device_id=(cross, to), device_id_type=MESH)
        if i:
            pl.semaphore_signal(barrier, inc=1, device_id=(g, to), device_id_type=MESH)
    pl.semaphore_wait(barrier, 2 * heads)

    def remote(src, dst, send_sem, recv_sem, to):
        return pltpu.make_async_remote_copy(
            src_ref=src, dst_ref=dst, send_sem=send_sem, recv_sem=recv_sem, device_id=to, device_id_type=MESH
        )

    def turn_of(i):
        return lax.rem(head + 1 + i, heads)

    def out_q(i):
        chunk = rows(turn_of(i), blocks * BLK)
        return remote(q_h.at[chunk], q_all.at[1, chunk], q_send.at[i], q_recv.at[i], (cross, head))

    out_t = remote(tables.at[1], lists_o, pair_send.at[0], pair_recv.at[0], (cross, head))
    out_v = remote(v_h, v_all.at[mine], pair_send.at[1], pair_recv.at[1], (mate, head))
    out_k = remote(k_h, k_all.at[mine], pair_send.at[2], pair_recv.at[2], (mate, head))
    out_t.start()
    out_v.start()
    out_k.start()
    for i in range(heads):
        out_q(i).start()
    in_v.wait()
    turn_values(v_all, vt, core * per_device, per_device)
    out_t.wait_recv()
    got_t = pltpu.make_async_copy(lists_o, tab.at[1], tab_sem.at[1])
    got_t.start()
    out_v.wait_recv()
    turn_values(v_all, vt, (1 - core) * per_device, per_device)
    in_k.wait()
    in_q.wait()
    in_t.wait()
    got_t.wait()
    out_k.wait_recv()

    def where_is(n):
        i = n // (2 * blocks)
        kind = 1 - n // blocks % 2
        return kind, turn_of(i) * blocks + n % blocks

    def slots_of(kind, b):
        line, at = b // (BLK // ROW), b % (BLK // ROW) * ROW
        ids = [tab[kind, line, at + j] for j in range(SLOTS)]
        bias = [tab[kind, SUBLINES + line, at + j].astype(F32) * -LOW for j in range(SLOTS)]
        return ids, bias

    def score(n, par):
        kind, b = where_is(n)
        ids, bias = slots_of(kind, b)
        return score_slots(q_all[kind, rows(b), :], k_all, s_ref, par, ids, bias)

    def weigh(n, par, top):
        kind, b = where_is(n)
        ids, bias = slots_of(kind, b)
        both = weigh_slots(s_ref, par, vt, ids, bias, top)
        sums = both[BLK : BLK + 8]
        sum0, sum1 = sums[:, :BLK], sums[:, BLK:]
        put_result(done.at[kind], b, both[0:HEAD_DIM, :BLK], both[HEAD_DIM:BLK, BLK:], top, sum0, sum1)

    def out_part(kind, i):
        to = turn_of(i)
        return remote(
            done.at[kind, pl.ds(to * blocks, blocks)], got.at[kind, i],
            part_send.at[kind, i], part_recv.at[kind, i], ((g, cross)[kind], to),
        )

    turns = 2 * heads * blocks // 2
    per_turn = turns // heads

    def pair(j, m0):
        i = j // per_turn
        at = lax.rem(j, per_turn)

        @pl.when(at == per_turn // 2)
        def _():
            out_part(1, i).start()

        @pl.when((at == 0) & (j > 0))
        def _():
            out_part(0, i - 1).start()

        @pl.when((at == per_turn - 1) & (i < heads - 1))
        def _():
            out_q(i + 1).wait_recv()

        n = 2 * j
        m1 = score(n + 1, 1)
        weigh(n, 0, m0)
        m2 = score(jnp.minimum(n + 2, 2 * turns - 1), 0)
        weigh(n + 1, 1, m1)
        return m2

    out_q(0).wait_recv()
    lax.fori_loop(0, turns, pair, score(0, 0))

    def join(i, own):
        out_part(1, i).wait_recv()
        source = lax.rem(head - 1 - i + 2 * heads, heads)
        for b in range(blocks):
            att[pl.ds(b * BLK, BLK), rows(source)] = combine((own(b), got[1, i, b]))

    def join_sent(i, carry):
        out_part(0, i).wait_recv()
        join(i, lambda b: got[0, i, b])
        return carry

    lax.fori_loop(0, heads - 1, join_sent, 0)
    join(heads - 1, lambda b: done[0, head * blocks + b])
    load_w.wait()

    size = blocks * BLK // SUBS

    def back(s, i):
        to = lax.rem(head + i, heads)
        return remote(
            stage.at[to, pl.ds(s * size, size)],
            home.at[pl.ds(pl.multiple_of(head * blocks * BLK, BLK) + s * size, size)],
            back_send.at[s, i], back_recv.at[s, i], (g, to),
        )

    for s in range(SUBS):
        for n in range(0, D, 256):
            out = jnp.dot(att[pl.ds(s * size, size), :], w_ref[:, n : n + 256], preferred_element_type=F32).astype(BF16)
            for c in range(2):
                stage[n // BLK + c, pl.ds(s * size, size), :] = out[:, c * BLK : (c + 1) * BLK]
        for i in range(1, heads):
            back(s, i).start()
        home[pl.ds(pl.multiple_of(head * blocks * BLK, BLK) + s * size, size), :] = stage[head, pl.ds(s * size, size), :]

    out_t.wait_send()
    out_v.wait_send()
    out_k.wait_send()
    for i in range(heads):
        out_q(i).wait_send()
        out_part(1, i).wait_send()
        if i < heads - 1:
            out_part(0, i).wait_send()
    for s in range(SUBS):
        for i in range(1, heads):
            back(s, i).wait()


def mixed_rows(tables, q, k, v, w_out):
    heads = lax.axis_size("head")
    per_device = k.shape[0]
    blocks = q.shape[0] // BLK // heads
    any_ = pl.BlockSpec(memory_space=pl.ANY)
    dma = pltpu.SemaphoreType.DMA
    return pl.pallas_call(
        mixed_kernel,
        out_shape=[jax.ShapeDtypeStruct(q.shape, BF16), jax.ShapeDtypeStruct(tables.shape[1:], I32)],
        in_specs=[any_] * 5,
        out_specs=[pl.BlockSpec(memory_space=pltpu.VMEM), any_],
        scratch_shapes=[
            pltpu.SMEM(tables.shape, I32),
            pltpu.VMEM((2,) + q.shape, BF16),
            pltpu.VMEM((2 * per_device, BLK, BLK), BF16),
            pltpu.VMEM((2 * per_device, BLK, BLK), BF16),
            pltpu.VMEM((2 * per_device, OUT, BLK), BF16),
            pltpu.VMEM((2, SLOTS * BLK, 2 * BLK), F32),
            pltpu.VMEM((2, heads * blocks, OUT, BLK), BF16),
            pltpu.VMEM((2, heads, blocks, OUT, BLK), BF16),
            pltpu.VMEM((blocks * BLK, D), BF16),
            pltpu.VMEM((D, D), BF16),
            pltpu.VMEM((heads, blocks * BLK, BLK), BF16),
            dma((2,)), dma((4,)), dma((3,)), dma((3,)), dma((heads,)), dma((heads,)),
            dma((2, heads)), dma((2, heads)), dma((SUBS, heads)), dma((SUBS, heads)),
        ],
        compiler_params=pltpu.CompilerParams(vmem_limit_bytes=56 << 20, collective_id=0, has_side_effects=True),
        name="mixed_rows",
    )(tables, q, k, v, w_out)[0]


def local(queries, resid, keys, values, w_out, block_lists, block_counts):
    per_device = keys.shape[0] // BLK
    keys, values = keys.reshape(-1, BLK, BLK), values.reshape(-1, BLK, BLK)
    g, core, mate, cross = place()
    used = jnp.arange(SLOTS, dtype=jnp.int32)[None, :] < block_counts[:, None]

    def table(first, count, base):
        here = block_lists - first * per_device
        on = used & (here >= 0) & (here < count * per_device)
        return jnp.stack([jnp.where(on, here + base, 0), 1 - on.astype(jnp.int32)])

    tables = jnp.stack([table(g - core, 2, 0), table(cross, 1, (1 - core) * per_device)])
    tables = jnp.pad(tables, ((0, 0), (0, 0), (0, 0), (0, ROW - SLOTS))).reshape(2, 2 * SUBLINES, BLK)
    home = mixed_rows(tables, queries, keys, values, w_out)
    return (resid.astype(jnp.float32) + home.astype(jnp.float32)).astype(jnp.bfloat16)


def solution(mesh):
    placed = (
        P("grid", "head"),
        P("grid", "head"),
        P("grid", "head"),
        P("grid", "head"),
        P(),
        P("grid", None),
        P("grid"),
    )
    return jax.shard_map(
        local, mesh=mesh, in_specs=placed, out_specs=P("grid", "head"), check_vma=False
    )
```

time: 358 us -> 85.3 us (0.24)
  the two profiles are of different devices: /device:TPU:24 before, /device:TPU:1 now
where the time goes in v3:
time: 85.3 us; the launch traced here: 85.1 us
  Pallas kernels  81.1 us (95%)
  other arithmetic  3.19 us (4%)
    pallas_call x1, Pallas kernels, mixed_rows(): pl.pallas_call(mixed_kernel, out_shape=[jax.ShapeDtypeStruct(q.shape, BF1...  81.1 us
    convert_element_type x1, other arithmetic, local(): (resid.astype(jnp.float32) + home.astype(jnp.float32)).astype(jnp.bfloat16)  2.47 us

profile of v3, /device:TPU:1, one launch (start us, length us, event | category | flops | bytes accessed | tf_op | source)
XLA Modules:
  0.0 85.1 jit_solution(10407054911297755526)
XLA Ops:
  0.0 0.7 select_bitcast_fusion.1
  0.7 0.1 copy.10
  0.9 0.7 reshape.10.tables
  1.5 0.0 copy-start
  1.5 81.1 %mixed_rows.1 = (bf16[4096,128]{1,0:T(8,128)(2,1)}, s32[8,128]{1,0:T(8,128)}) custom-call(s32[2,8,128]{2,1,0:T(8,128)} %reshape.10.tables, bf16[4096,128]{1,0:T(8,128)(2,1)} %q_h.1, bf16[48,128,128]{2,1,0:T(8,128)(2,1)} %bitcast.16, bf16[48,128,128]{2,1,0:T(8,128)(2,1)} %bitcast.17, bf16[1024,1024]{1,0:T(8,128)(2,1)} %w_h.1), custom_call_target="tpu_custom_call" | custom-call | tf_op jit(solution)/shard_map/mixed_rows/pallas_call | solution.py:281
  82.7 0.0 copy-done
  82.7 2.5 %add_convert_fusion = bf16[4096,128]{1,0:T(8,128)(2,1)} fusion(bf16[4096,128]{1,0:T(8,128)(2,1)} %get-tuple-element.6, bf16[4096,128]{1,0:T(8,128)(2,1)S(1)} %copy-done), kind=kLoop, calls=%fused_computation | loop fusion | flops 2097152 | bytes 3145728 | tf_op jit(solution)/shard_map/convert_element_type | solution.py:320
  (3 shorter events, 0.0 us)
Async XLA Ops:
  1.5 81.1 %copy-start = (bf16[4096,128]{1,0:T(8,128)(2,1)S(1)}, bf16[4096,128]{1,0:T(8,128)(2,1)}, u32[]{:S(2)}) copy-start(bf16[4096,128]{1,0:T(8,128)(2,1)} %param.8) | copy-start | bytes 3145732

commit v4 on v3

v4 whole, which is shorter than its diff:
```python
import functools
import math

import jax
import jax.numpy as jnp
from jax import lax
from jax.experimental import pallas as pl
from jax.experimental.pallas import tpu as pltpu
from jax.sharding import PartitionSpec as P

D = 1024
HEADS = 16
HEAD_DIM = D // HEADS
BLK = 128
SLOTS = 12
ROW = 16
OUT = BLK + 16
LOG2 = math.log2(math.e) / math.sqrt(HEAD_DIM)
LOW = -1e30
SUBLINES = 4
SUBS = 2
PER = 2
UNIT = PER * BLK + 16
CROSS_ORDER = ((0, 1), (1, 3), (0, 2), (1, 1), (0, 3), (1, 0), (1, 2), (0, 0))
OWN_ORDER = ((1, 3), (0, 2), (1, 1), (0, 3), (1, 0), (0, 1), (1, 2), (0, 0))
MIDDLE = 24
BF16, F32, I32 = jnp.bfloat16, jnp.float32, jnp.int32
MESH = pl.DeviceIdType.MESH


def rows(b, size=BLK):
    return pl.ds(pl.multiple_of(b * size, size), size)


def place():
    count = lax.axis_size("grid")
    g = lax.axis_index("grid")
    core = lax.rem(g, 2)
    return g, core, g + 1 - 2 * core, lax.rem(g - 1 + 2 * core + count, count)


def both_heads(q):
    qt = q.T
    row = lax.broadcasted_iota(I32, (BLK, BLK), 0)
    zero = jnp.zeros_like(qt)
    return jnp.concatenate([jnp.where(row < HEAD_DIM, qt, zero), jnp.where(row >= HEAD_DIM, qt, zero)], axis=1)


def score_slots(q, k_ref, s_ref, par, ids, bias):
    q_both = both_heads(q)
    top = None
    for j, (c, less) in enumerate(zip(ids, bias)):
        s = jnp.dot(k_ref[c], q_both, preferred_element_type=F32)
        s_ref[par, pl.ds(j * BLK, BLK), :] = s
        m = jnp.max(s.reshape(BLK // 8, 8, 2 * BLK), axis=0)
        m = m - less
        top = m if top is None else jnp.maximum(top, m)
    top = jnp.max(top, axis=0, keepdims=True) * LOG2
    return top.astype(BF16).astype(F32)


def weigh_slots(s_ref, par, vt, ids, bias, top):
    both = None
    for j in range(0, len(ids), 2):
        w = []
        for i in (j, j + 1):
            shift = top + bias[i]
            w.append(jnp.exp2(s_ref[par, pl.ds(i * BLK, BLK), :] * LOG2 - shift).astype(BF16))
        vals = jnp.concatenate([vt[ids[j]], vt[ids[j + 1]]], axis=1)
        d = jnp.dot(vals, jnp.concatenate(w, axis=0), preferred_element_type=F32)
        both = d if both is None else both + d
    return both


def turn_values(v_ref, vt, first, count):
    def turn(i, carry):
        c = first + i
        vt[c, 0:BLK, :] = v_ref[c].T
        vt[c, BLK:OUT, :] = jnp.ones((OUT - BLK, BLK), BF16)
        return carry

    lax.fori_loop(0, count, turn, 0, unroll=4)


def put_sums(o_ref, at, block, both):
    o_ref[at, block * BLK : block * BLK + HEAD_DIM] = both[0:HEAD_DIM, :BLK].astype(BF16)
    o_ref[at, block * BLK + HEAD_DIM : (block + 1) * BLK] = both[HEAD_DIM:BLK, BLK:].astype(BF16)


def put_stats(o_ref, at, tops, sums):
    row = lax.broadcasted_iota(I32, (16, BLK), 0)
    stats = jnp.zeros((16, BLK), F32)
    for block, (top, total) in enumerate(zip(tops, sums)):
        high = total.astype(BF16).astype(F32)
        for h in range(2):
            part = slice(h * BLK, (h + 1) * BLK)
            for i, line in enumerate((top, high, total - high)):
                stats = jnp.where(row == 6 * block + 3 * h + i, line[0:1, part], stats)
    o_ref[at, PER * BLK : UNIT] = stats.astype(BF16)


def combine(parts, block):
    stats = [p[PER * BLK : UNIT].astype(F32) for p in parts]
    heads = []
    for h in range(2):
        at = 6 * block + 3 * h
        sums = [s[at + 1 : at + 2] + s[at + 2 : at + 3] for s in stats]
        tops = [jnp.where(l > 0, s[at : at + 1], LOW) for s, l in zip(stats, sums)]
        top = functools.reduce(jnp.maximum, tops)
        scale = [jnp.exp2(t - top) for t in tops]
        total = sum(l * c for l, c in zip(sums, scale))
        part = slice(block * BLK + h * HEAD_DIM, block * BLK + (h + 1) * HEAD_DIM)
        heads.append(sum(p[part].astype(F32) * (c / total) for p, c in zip(parts, scale)))
    return jnp.concatenate(heads, axis=0).T.astype(BF16)


def mixed_kernel(
    tables, q_h, k_h, v_h, w_h, resid_h, out, lists_o,
    tab, q_all, k_all, v_all, vt, s_ref, done, got, att, w_ref, stage, home, resid,
    tab_sem, load_sem, out_sem, pair_send, pair_recv, q_send, q_recv, part_send, part_recv, back_send, back_recv,
):
    heads = lax.axis_size("head")
    head = lax.axis_index("head")
    g, core, mate, cross = place()
    per_device = k_h.shape[0]
    blocks = q_h.shape[0] // BLK // heads
    load_w = pltpu.make_async_copy(w_h, w_ref, load_sem.at[0])
    mine = pl.ds(core * per_device, per_device)
    in_v = pltpu.make_async_copy(v_h, v_all.at[mine], load_sem.at[1])
    in_k = pltpu.make_async_copy(k_h, k_all.at[mine], load_sem.at[2])
    in_q = pltpu.make_async_copy(q_h, q_all.at[0], load_sem.at[3])
    in_r = pltpu.make_async_copy(resid_h, resid, load_sem.at[4])
    in_t = pltpu.make_async_copy(tables.at[0], tab.at[0], tab_sem.at[0])
    for load in (in_v, in_t, in_q, in_k, load_w, in_r):
        load.start()

    barrier = pltpu.get_barrier_semaphore()
    pl.semaphore_signal(barrier, inc=1, device_id=(mate, head), device_id_type=MESH)
    for i in range(heads):
        to = lax.rem(head + i, heads)
        pl.semaphore_signal(barrier, inc=1, device_id=(cross, to), device_id_type=MESH)
        if i:
            pl.semaphore_signal(barrier, inc=1, device_id=(g, to), device_id_type=MESH)
    pl.semaphore_wait(barrier, 2 * heads)

    def remote(src, dst, send_sem, recv_sem, to):
        return pltpu.make_async_remote_copy(
            src_ref=src, dst_ref=dst, send_sem=send_sem, recv_sem=recv_sem, device_id=to, device_id_type=MESH
        )

    def turn_of(kind, i):
        x = sum((i == n).astype(I32) * (kind * CROSS_ORDER[n][0] + (1 - kind) * OWN_ORDER[n][0]) for n in range(8))
        z = sum((i == n).astype(I32) * (kind * CROSS_ORDER[n][1] + (1 - kind) * OWN_ORDER[n][1]) for n in range(8))
        return lax.rem(head // 4 + x, 2) * 4 + lax.rem(head % 4 + z, 4)

    def out_q(s, i):
        chunk = rows(turn_of(1, i) * SUBS + s, PER * BLK)
        return remote(q_h.at[chunk], q_all.at[1, chunk], q_send.at[s, i], q_recv.at[s, i], (cross, head))

    out_t = remote(tables.at[1], lists_o, pair_send.at[0], pair_recv.at[0], (cross, head))
    out_v = remote(v_h, v_all.at[mine], pair_send.at[1], pair_recv.at[1], (mate, head))
    out_k = remote(k_h, k_all.at[mine], pair_send.at[2], pair_recv.at[2], (mate, head))
    out_t.start()
    out_v.start()
    out_k.start()
    for s in range(SUBS):
        def send_q(i, carry):
            out_q(s, i).start()
            return carry

        lax.fori_loop(0, heads, send_q, 0)
    in_v.wait()
    turn_values(v_all, vt, core * per_device, per_device)
    out_t.wait_recv()
    got_t = pltpu.make_async_copy(lists_o, tab.at[1], tab_sem.at[1])
    got_t.start()
    out_v.wait_recv()
    turn_values(v_all, vt, (1 - core) * per_device, per_device)
    in_k.wait()
    in_q.wait()
    in_t.wait()
    got_t.wait()
    out_k.wait_recv()

    turns = 2 * heads * SUBS

    def part_of(j):
        i = lax.rem(j // 2, heads)
        kind = 1 - lax.rem(j, 2)
        return kind, j // (2 * heads), i

    def slots_of(kind, b):
        line, at = b // (BLK // ROW), b % (BLK // ROW) * ROW
        ids = [tab[kind, line, at + j] for j in range(SLOTS)]
        bias = [tab[kind, SUBLINES + line, at + j].astype(F32) * -LOW for j in range(SLOTS)]
        return ids, bias

    def score(kind, b, par):
        ids, bias = slots_of(kind, b)
        return score_slots(q_all[kind, rows(b), :], k_all, s_ref, par, ids, bias)

    def weigh(kind, b, par, top, at, block):
        ids, bias = slots_of(kind, b)
        both = weigh_slots(s_ref, par, vt, ids, bias, top)
        put_sums(done.at[kind], at, block, both)
        return both[BLK : BLK + 1]

    def out_part(kind, s, i):
        to = turn_of(kind, i)
        return remote(
            done.at[kind, to * SUBS + s], got.at[kind, s, head],
            part_send.at[kind, s, i], part_recv.at[kind, s, i], ((g, cross)[kind], to),
        )

    size = PER * BLK

    def back(s, i):
        to = lax.rem(head + i, heads)
        return remote(
            stage.at[to, pl.ds(s * size, size)], home.at[head, pl.ds(s * size, size)],
            back_send.at[s, i], back_recv.at[s, i], (g, to),
        )

    def project(s):
        def join(i, carry):
            out_part(1, s, i).wait_recv()
            return carry

        def join_own(i, carry):
            out_part(0, s, i).wait_recv()
            return carry

        lax.fori_loop(0, heads, join, 0)
        lax.fori_loop(0, heads - 1, join_own, 0)

        def mix(source, carry):
            for b in range(PER):
                att[pl.ds(s * size + b * BLK, BLK), rows(source)] = combine(
                    (got.at[0, s, source], got.at[1, s, source]), b
                )
            return carry

        lax.fori_loop(0, heads, mix, 0)
        for n in range(0, D, 256):
            res = jnp.dot(att[pl.ds(s * size, size), :], w_ref[:, n : n + 256], preferred_element_type=F32).astype(BF16)
            for c in range(2):
                stage[n // BLK + c, pl.ds(s * size, size), :] = res[:, c * BLK : (c + 1) * BLK]
        for i in range(1, heads):
            back(s, i).start()

    def pair(j, m0):
        kind, s, i = part_of(j)

        @pl.when(kind == 0)
        def _():
            out_part(1, s, i).start()

        @pl.when((kind == 1) & (i > 0))
        def _():
            out_part(0, s, i - 1).start()

        @pl.when((kind == 1) & (i == 0) & (j > 0))
        def _():
            keep = pltpu.make_async_copy(done.at[0, head * SUBS], got.at[0, 0, head], out_sem.at[0])
            keep.start()
            keep.wait()

        @pl.when(j == MIDDLE)
        def _():
            load_w.wait()
            project(0)

        after = jnp.minimum(j + 1, turns - 1)
        kind2, s2, i2 = part_of(after)

        @pl.when((kind2 == 1) & (j < turns - 1))
        def _():
            out_q(s2, i2).wait_recv()

        to = turn_of(kind, i)
        b = (to * SUBS + s) * PER
        m1 = score(kind, b + 1, 1)
        l0 = weigh(kind, b, 0, m0, to * SUBS + s, 0)
        m2 = score(kind2, (turn_of(kind2, i2) * SUBS + s2) * PER, 0)
        l1 = weigh(kind, b + 1, 1, m1, to * SUBS + s, 1)
        put_stats(done.at[kind], to * SUBS + s, (m0, m1), (l0, l1))
        return m2

    zero = jnp.int32(0)
    out_q(zero, zero).wait_recv()
    lax.fori_loop(0, turns, pair, score(1, turn_of(1, zero) * SUBS * PER, 0))
    keep = pltpu.make_async_copy(done.at[0, head * SUBS + 1], got.at[0, 1, head], out_sem.at[0])
    keep.start()
    keep.wait()
    project(1)

    def finish(s, i):
        source = lax.rem(head - i + heads, heads)
        where = rows(source * SUBS + s, size)
        if i:
            back(s, i).wait_recv()
            come = home[source, pl.ds(s * size, size), :]
        else:
            come = stage[head, pl.ds(s * size, size), :]
        resid[where, :] = (resid[where, :].astype(F32) + come.astype(F32)).astype(BF16)
        return pltpu.make_async_copy(resid.at[where], out.at[where], out_sem.at[s * heads + i])

    in_r.wait()
    for s in range(SUBS):
        for i in range(heads):
            finish_copy = finish(s, i)
            finish_copy.start()

    out_t.wait_send()
    out_v.wait_send()
    out_k.wait_send()

    for s in range(SUBS):
        def sent(i, carry):
            out_q(s, i).wait_send()
            out_part(1, s, i).wait_send()
            return carry

        def sent_own(i, carry):
            out_part(0, s, i).wait_send()
            return carry

        lax.fori_loop(0, heads, sent, 0)
        lax.fori_loop(0, heads - 1, sent_own, 0)
        for i in range(heads):
            if i:
                back(s, i).wait_send()
            source = lax.rem(head - i + heads, heads)
            where = rows(source * SUBS + s, size)
            pltpu.make_async_copy(resid.at[where], out.at[where], out_sem.at[s * heads + i]).wait()


def mixed_rows(tables, q, k, v, w_out, resid):
    heads = lax.axis_size("head")
    per_device = k.shape[0]
    blocks = q.shape[0] // BLK // heads
    any_ = pl.BlockSpec(memory_space=pl.ANY)
    dma = pltpu.SemaphoreType.DMA
    return pl.pallas_call(
        mixed_kernel,
        out_shape=[jax.ShapeDtypeStruct(q.shape, BF16), jax.ShapeDtypeStruct(tables.shape[1:], I32)],
        in_specs=[any_] * 6,
        out_specs=[any_, any_],
        scratch_shapes=[
            pltpu.SMEM(tables.shape, I32),
            pltpu.VMEM((2,) + q.shape, BF16),
            pltpu.VMEM((2 * per_device, BLK, BLK), BF16),
            pltpu.VMEM((2 * per_device, BLK, BLK), BF16),
            pltpu.VMEM((2 * per_device, OUT, BLK), BF16),
            pltpu.VMEM((2, SLOTS * BLK, 2 * BLK), F32),
            pltpu.VMEM((2, heads * SUBS, UNIT, BLK), BF16),
            pltpu.VMEM((2, SUBS, heads, UNIT, BLK), BF16),
            pltpu.VMEM((blocks * BLK, D), BF16),
            pltpu.VMEM((D, D), BF16),
            pltpu.VMEM((heads, blocks * BLK, BLK), BF16),
            pltpu.VMEM((heads, blocks * BLK, BLK), BF16),
            pltpu.VMEM(q.shape, BF16),
            dma((2,)), dma((5,)), dma((SUBS * heads,)), dma((3,)), dma((3,)), dma((SUBS, heads)), dma((SUBS, heads)),
            dma((2, SUBS, heads)), dma((2, SUBS, heads)), dma((SUBS, heads)), dma((SUBS, heads)),
        ],
        compiler_params=pltpu.CompilerParams(vmem_limit_bytes=56 << 20, collective_id=0, has_side_effects=True),
        name="mixed_rows",
    )(tables, q, k, v, w_out, resid)[0]


def local(queries, resid, keys, values, w_out, block_lists, block_counts):
    per_device = keys.shape[0] // BLK
    keys, values = keys.reshape(-1, BLK, BLK), values.reshape(-1, BLK, BLK)
    g, core, mate, cross = place()
    used = jnp.arange(SLOTS, dtype=jnp.int32)[None, :] < block_counts[:, None]

    def table(first, count, base):
        here = block_lists - first * per_device
        on = used & (here >= 0) & (here < count * per_device)
        return jnp.stack([jnp.where(on, here + base, 0), 1 - on.astype(jnp.int32)])

    tables = jnp.stack([table(g - core, 2, 0), table(cross, 1, (1 - core) * per_device)])
    tables = jnp.pad(tables, ((0, 0), (0, 0), (0, 0), (0, ROW - SLOTS))).reshape(2, 2 * SUBLINES, BLK)
    return mixed_rows(tables, queries, keys, values, w_out, resid)


def solution(mesh):
    placed = (
        P("grid", "head"),
        P("grid", "head"),
        P("grid", "head"),
        P("grid", "head"),
        P(),
        P("grid", None),
        P("grid"),
    )
    return jax.shard_map(
        local, mesh=mesh, in_specs=placed, out_specs=P("grid", "head"), check_vma=False
    )
```

time: 85.3 us -> 78.8 us (0.924)
  the two profiles are of different devices: /device:TPU:1 before, /device:TPU:24 now
where the time goes in v4:
time: 78.8 us; the launch traced here: 78.5 us
  Pallas kernels  74.7 us (95%)
  local copies, waits for them, and re-layouts  3.06 us (4%)
    pallas_call x1, Pallas kernels, mixed_rows(): pl.pallas_call(mixed_kernel, out_shape=[jax.ShapeDtypeStruct(q.shape, BF1...  74.7 us
    unnamed x2, local copies, waits for them, and re-layouts  2.37 us

profile of v4, /device:TPU:24, one launch (start us, length us, event | category | flops | bytes accessed | tf_op | source)
XLA Modules:
  0.0 78.5 jit_solution(18286921908989793782)
XLA Ops:
  0.0 0.7 select_bitcast_fusion.1
  0.7 0.1 copy.10
  0.9 0.7 reshape.10.tables
  1.5 74.7 %mixed_rows.1 = (bf16[4096,128]{1,0:T(8,128)(2,1)}, s32[8,128]{1,0:T(8,128)}) custom-call(s32[2,8,128]{2,1,0:T(8,128)} %reshape.10.tables, bf16[4096,128]{1,0:T(8,128)(2,1)} %q_h.1, bf16[48,128,128]{2,1,0:T(8,128)(2,1)} %bitcast.16, bf16[48,128,128]{2,1,0:T(8,128)(2,1)} %bitcast.17, bf16[1024,1024]{1,0:T(8,128)(2,1)} %w_h.1, bf16[4096,128]{1,0:T(8,128)(2,1)} %resid_h.1), custom_call_target="tpu_custom_call" | custom-call | tf_op jit(solution)/shard_map/mixed_rows/pallas_call | solution.py:344
  76.2 2.3 %copy.12 = bf16[4096,128]{1,0:T(8,128)(2,1)} copy(bf16[4096,128]{1,0:T(8,128)(2,1)} %get-tuple-element.6) | data formatting | bytes 2097152
  (3 shorter events, 0.0 us)

commit v5 on v4

--- a/solution.py
+++ b/solution.py
@@ -13,17 +13,14 @@
 HEAD_DIM = D // HEADS
 BLK = 128
 SLOTS = 12
-ROW = 16
 OUT = BLK + 16
 LOG2 = math.log2(math.e) / math.sqrt(HEAD_DIM)
 LOW = -1e30
-SUBLINES = 4
 SUBS = 2
 PER = 2
 UNIT = PER * BLK + 16
 CROSS_ORDER = ((0, 1), (1, 3), (0, 2), (1, 1), (0, 3), (1, 0), (1, 2), (0, 0))
-OWN_ORDER = ((1, 3), (0, 2), (1, 1), (0, 3), (1, 0), (0, 1), (1, 2), (0, 0))
-MIDDLE = 24
+OWN_ORDER = ((0, 1), (0, 3), (0, 2), (1, 0), (1, 1), (1, 3), (1, 2), (0, 0))
 BF16, F32, I32 = jnp.bfloat16, jnp.float32, jnp.int32
 MESH = pl.DeviceIdType.MESH
 
@@ -115,8 +112,8 @@
 
 
 def mixed_kernel(
-    tables, q_h, k_h, v_h, w_h, resid_h, out, lists_o,
-    tab, q_all, k_all, v_all, vt, s_ref, done, got, att, w_ref, stage, home, resid,
+    lists_h, counts_h, q_h, k_h, v_h, w_h, resid_h, out,
+    lists, counts, made, came, tab, q_all, k_all, v_all, vt, s_ref, done, got, att, w_ref, stage, home, resid,
     tab_sem, load_sem, out_sem, pair_send, pair_recv, q_send, q_recv, part_send, part_recv, back_send, back_recv,
 ):
     heads = lax.axis_size("head")
@@ -130,8 +127,9 @@
     in_k = pltpu.make_async_copy(k_h, k_all.at[mine], load_sem.at[2])
     in_q = pltpu.make_async_copy(q_h, q_all.at[0], load_sem.at[3])
     in_r = pltpu.make_async_copy(resid_h, resid, load_sem.at[4])
-    in_t = pltpu.make_async_copy(tables.at[0], tab.at[0], tab_sem.at[0])
-    for load in (in_v, in_t, in_q, in_k, load_w, in_r):
+    in_l = pltpu.make_async_copy(lists_h, lists, tab_sem.at[2])
+    in_c = pltpu.make_async_copy(counts_h, counts, tab_sem.at[3])
+    for load in (in_l, in_c, in_v, in_q, in_k, load_w, in_r):
         load.start()
 
     barrier = pltpu.get_barrier_semaphore()
@@ -141,6 +139,18 @@
         pl.semaphore_signal(barrier, inc=1, device_id=(cross, to), device_id_type=MESH)
         if i:
             pl.semaphore_signal(barrier, inc=1, device_id=(g, to), device_id_type=MESH)
+
+    made[...] = jnp.zeros_like(made)
+    in_l.wait()
+    in_c.wait()
+    used = lax.broadcasted_iota(I32, lists.shape, 0) < counts[...]
+    for n, (first, count, base) in enumerate(((g - core, 2, 0), (cross, 1, (1 - core) * per_device))):
+        here = lists[...] - first * per_device
+        on = used & (here >= 0) & (here < count * per_device)
+        made[n, 0, 0:SLOTS, 0 : lists.shape[1]] = jnp.where(on, here + base, 0)
+        made[n, 1, 0:SLOTS, 0 : lists.shape[1]] = jnp.where(on, 0, 1)
+    in_t = pltpu.make_async_copy(made.at[0], tab.at[0], tab_sem.at[0])
+    in_t.start()
     pl.semaphore_wait(barrier, 2 * heads)
 
     def remote(src, dst, send_sem, recv_sem, to):
@@ -157,7 +167,7 @@
         chunk = rows(turn_of(1, i) * SUBS + s, PER * BLK)
         return remote(q_h.at[chunk], q_all.at[1, chunk], q_send.at[s, i], q_recv.at[s, i], (cross, head))
 
-    out_t = remote(tables.at[1], lists_o, pair_send.at[0], pair_recv.at[0], (cross, head))
+    out_t = remote(made.at[1], came, pair_send.at[0], pair_recv.at[0], (cross, head))
     out_v = remote(v_h, v_all.at[mine], pair_send.at[1], pair_recv.at[1], (mate, head))
     out_k = remote(k_h, k_all.at[mine], pair_send.at[2], pair_recv.at[2], (mate, head))
     out_t.start()
@@ -172,7 +182,7 @@
     in_v.wait()
     turn_values(v_all, vt, core * per_device, per_device)
     out_t.wait_recv()
-    got_t = pltpu.make_async_copy(lists_o, tab.at[1], tab_sem.at[1])
+    got_t = pltpu.make_async_copy(came, tab.at[1], tab_sem.at[1])
     got_t.start()
     out_v.wait_recv()
     turn_values(v_all, vt, (1 - core) * per_device, per_device)
@@ -185,14 +195,16 @@
     turns = 2 * heads * SUBS
 
     def part_of(j):
-        i = lax.rem(j // 2, heads)
-        kind = 1 - lax.rem(j, 2)
-        return kind, j // (2 * heads), i
+        s, at = j // (2 * heads), lax.rem(j, 2 * heads)
+        third, group = lax.rem(at, 3), at // 3 - 1
+        mixed = (at >= 3) & (at < 15)
+        kind = (mixed & (third < 2)).astype(I32)
+        i = jnp.where(kind == 1, 2 * group + third, jnp.where(mixed, 3 + group, jnp.where(at < 3, at, heads - 1)))
+        return kind, s, i
 
     def slots_of(kind, b):
-        line, at = b // (BLK // ROW), b % (BLK // ROW) * ROW
-        ids = [tab[kind, line, at + j] for j in range(SLOTS)]
-        bias = [tab[kind, SUBLINES + line, at + j].astype(F32) * -LOW for j in range(SLOTS)]
+        ids = [tab[kind, 0, j, b] for j in range(SLOTS)]
+        bias = [tab[kind, 1, j, b].astype(F32) * -LOW for j in range(SLOTS)]
         return ids, bias
 
     def score(kind, b, par):
@@ -214,11 +226,11 @@
 
     size = PER * BLK
 
-    def back(s, i):
+    def back(b, i):
         to = lax.rem(head + i, heads)
         return remote(
-            stage.at[to, pl.ds(s * size, size)], home.at[head, pl.ds(s * size, size)],
-            back_send.at[s, i], back_recv.at[s, i], (g, to),
+            stage.at[to, pl.ds(b * BLK, BLK)], home.at[head, pl.ds(b * BLK, BLK)],
+            back_send.at[b, i], back_recv.at[b, i], (g, to),
         )
 
     def project(s):
@@ -233,42 +245,39 @@
         lax.fori_loop(0, heads, join, 0)
         lax.fori_loop(0, heads - 1, join_own, 0)
 
-        def mix(source, carry):
-            for b in range(PER):
-                att[pl.ds(s * size + b * BLK, BLK), rows(source)] = combine(
-                    (got.at[0, s, source], got.at[1, s, source]), b
-                )
-            return carry
-
-        lax.fori_loop(0, heads, mix, 0)
-        for n in range(0, D, 256):
-            res = jnp.dot(att[pl.ds(s * size, size), :], w_ref[:, n : n + 256], preferred_element_type=F32).astype(BF16)
-            for c in range(2):
-                stage[n // BLK + c, pl.ds(s * size, size), :] = res[:, c * BLK : (c + 1) * BLK]
-        for i in range(1, heads):
-            back(s, i).start()
+        for n in range(PER):
+            b = s * PER + n
+
+            def mix(source, carry):
+                att[pl.ds(b * BLK, BLK), rows(source)] = combine((got.at[0, s, source], got.at[1, s, source]), n)
+                return carry
+
+            lax.fori_loop(0, heads, mix, 0, unroll=2)
+            for c in range(0, heads, 2):
+                res = jnp.dot(att[pl.ds(b * BLK, BLK), :], w_ref[:, c * BLK : (c + 2) * BLK], preferred_element_type=F32)
+                for d in range(2):
+                    stage[c + d, pl.ds(b * BLK, BLK), :] = res[:, d * BLK : (d + 1) * BLK].astype(BF16)
+            for i in range(1, heads):
+                back(b, i).start()
 
     def pair(j, m0):
         kind, s, i = part_of(j)
 
-        @pl.when(kind == 0)
+        kind1, s1, i1 = part_of(jnp.maximum(j - 1, 0))
+
+        @pl.when((j > 0) & (kind1 == 1))
         def _():
-            out_part(1, s, i).start()
-
-        @pl.when((kind == 1) & (i > 0))
+            out_part(1, s1, i1).start()
+
+        @pl.when((j > 0) & (kind1 == 0) & (i1 < heads - 1))
         def _():
-            out_part(0, s, i - 1).start()
-
-        @pl.when((kind == 1) & (i == 0) & (j > 0))
+            out_part(0, s1, i1).start()
+
+        @pl.when(j == 2 * heads)
         def _():
             keep = pltpu.make_async_copy(done.at[0, head * SUBS], got.at[0, 0, head], out_sem.at[0])
             keep.start()
             keep.wait()
-
-        @pl.when(j == MIDDLE)
-        def _():
-            load_w.wait()
-            project(0)
 
         after = jnp.minimum(j + 1, turns - 1)
         kind2, s2, i2 = part_of(after)
@@ -287,18 +296,20 @@
         return m2
 
     zero = jnp.int32(0)
-    out_q(zero, zero).wait_recv()
-    lax.fori_loop(0, turns, pair, score(1, turn_of(1, zero) * SUBS * PER, 0))
+    lax.fori_loop(0, turns, pair, score(0, turn_of(0, zero) * SUBS * PER, 0))
     keep = pltpu.make_async_copy(done.at[0, head * SUBS + 1], got.at[0, 1, head], out_sem.at[0])
     keep.start()
     keep.wait()
+    load_w.wait()
+    project(0)
     project(1)
 
     def finish(s, i):
         source = lax.rem(head - i + heads, heads)
         where = rows(source * SUBS + s, size)
         if i:
-            back(s, i).wait_recv()
+            for n in range(PER):
+                back(s * PER + n, i).wait_recv()
             come = home[source, pl.ds(s * size, size), :]
         else:
             come = stage[head, pl.ds(s * size, size), :]
@@ -329,13 +340,14 @@
         lax.fori_loop(0, heads - 1, sent_own, 0)
         for i in range(heads):
             if i:
-                back(s, i).wait_send()
+                for n in range(PER):
+                    back(s * PER + n, i).wait_send()
             source = lax.rem(head - i + heads, heads)
             where = rows(source * SUBS + s, size)
             pltpu.make_async_copy(resid.at[where], out.at[where], out_sem.at[s * heads + i]).wait()
 
 
-def mixed_rows(tables, q, k, v, w_out, resid):
+def mixed_rows(lists, counts, q, k, v, w_out, resid):
     heads = lax.axis_size("head")
     per_device = k.shape[0]
     blocks = q.shape[0] // BLK // heads
@@ -343,11 +355,15 @@
     dma = pltpu.SemaphoreType.DMA
     return pl.pallas_call(
         mixed_kernel,
-        out_shape=[jax.ShapeDtypeStruct(q.shape, BF16), jax.ShapeDtypeStruct(tables.shape[1:], I32)],
-        in_specs=[any_] * 6,
-        out_specs=[any_, any_],
+        out_shape=jax.ShapeDtypeStruct(q.shape, BF16),
+        in_specs=[any_] * 7,
+        out_specs=any_,
         scratch_shapes=[
-            pltpu.SMEM(tables.shape, I32),
+            pltpu.VMEM(lists.shape, I32),
+            pltpu.VMEM(counts.shape, I32),
+            pltpu.VMEM((2, 2, 16, BLK), I32),
+            pltpu.VMEM((2, 16, BLK), I32),
+            pltpu.SMEM((2, 2, 16, BLK), I32),
             pltpu.VMEM((2,) + q.shape, BF16),
             pltpu.VMEM((2 * per_device, BLK, BLK), BF16),
             pltpu.VMEM((2 * per_device, BLK, BLK), BF16),
@@ -360,28 +376,17 @@
             pltpu.VMEM((heads, blocks * BLK, BLK), BF16),
             pltpu.VMEM((heads, blocks * BLK, BLK), BF16),
             pltpu.VMEM(q.shape, BF16),
-            dma((2,)), dma((5,)), dma((SUBS * heads,)), dma((3,)), dma((3,)), dma((SUBS, heads)), dma((SUBS, heads)),
-            dma((2, SUBS, heads)), dma((2, SUBS, heads)), dma((SUBS, heads)), dma((SUBS, heads)),
+            dma((4,)), dma((5,)), dma((SUBS * heads,)), dma((3,)), dma((3,)), dma((SUBS, heads)), dma((SUBS, heads)),
+            dma((2, SUBS, heads)), dma((2, SUBS, heads)), dma((blocks, heads)), dma((blocks, heads)),
         ],
-        compiler_params=pltpu.CompilerParams(vmem_limit_bytes=56 << 20, collective_id=0, has_side_effects=True),
+        compiler_params=pltpu.CompilerParams(vmem_limit_bytes=52 << 20, collective_id=0, has_side_effects=True),
         name="mixed_rows",
-    )(tables, q, k, v, w_out, resid)[0]
+    )(lists, counts, q, k, v, w_out, resid)
 
 
 def local(queries, resid, keys, values, w_out, block_lists, block_counts):
-    per_device = keys.shape[0] // BLK
     keys, values = keys.reshape(-1, BLK, BLK), values.reshape(-1, BLK, BLK)
-    g, core, mate, cross = place()
-    used = jnp.arange(SLOTS, dtype=jnp.int32)[None, :] < block_counts[:, None]
-
-    def table(first, count, base):
-        here = block_lists - first * per_device
-        on = used & (here >= 0) & (here < count * per_device)
-        return jnp.stack([jnp.where(on, here + base, 0), 1 - on.astype(jnp.int32)])
-
-    tables = jnp.stack([table(g - core, 2, 0), table(cross, 1, (1 - core) * per_device)])
-    tables = jnp.pad(tables, ((0, 0), (0, 0), (0, 0), (0, ROW - SLOTS))).reshape(2, 2 * SUBLINES, BLK)
-    return mixed_rows(tables, queries, keys, values, w_out, resid)
+    return mixed_rows(block_lists.T, block_counts[None, :], queries, keys, values, w_out, resid)
 
 
 def solution(mesh):

time: 78.8 us -> 72.8 us (0.924)
  Pallas kernels: 74.7 us -> 70.1 us
    pallas_call x1, Pallas kernels: 74.7 us -> 70.1 us  [mixed_rows(): pl.pallas_call(mixed_kernel, out_shape=jax.ShapeDtypeStruct(q.shape, BF16...]
    unnamed x2 -> x5, local copies, waits for them, and re-layouts: 2.37 us -> 2.32 us
where the time goes in v5:
time: 72.8 us; the launch traced here: 72.4 us
  Pallas kernels  70.1 us (96%)
  local copies, waits for them, and re-layouts  2.32 us (3%)
    pallas_call x1, Pallas kernels, mixed_rows(): pl.pallas_call(mixed_kernel, out_shape=jax.ShapeDtypeStruct(q.shape, BF16...  70.1 us
    unnamed x5, local copies, waits for them, and re-layouts  2.32 us

profile of v5, /device:TPU:24, one launch (start us, length us, event | category | flops | bytes accessed | tf_op | source)
XLA Modules:
  0.0 72.4 jit_solution(51427727228440948)
XLA Ops:
  0.0 0.0 copy-start
  0.0 0.7 copy-done
  0.7 0.0 copy-start.1
  0.7 0.7 copy-done.1
  1.4 70.1 %mixed_rows.1 = bf16[4096,128]{1,0:T(8,128)(2,1)S(1)} custom-call(s32[12,32]{1,0:T(8,128)S(1)} %bitcast.4, s32[1,32]{1,0:T(1,128)S(1)} %bitcast.5, bf16[4096,128]{1,0:T(8,128)(2,1)} %q_h.1, bf16[48,128,128]{2,1,0:T(8,128)(2,1)} %bitcast.6, bf16[48,128,128]{2,1,0:T(8,128)(2,1)} %bitcast.7, bf16[1024,1024]{1,0:T(8,128)(2,1)} %w_h.1, bf16[4096,128]{1,0:T(8,128)(2,1)} %resid_h.1), custom_call_target="tpu_custom_call" | custom-call | tf_op jit(solution)/shard_map/mixed_rows/pallas_call | solution.py:356
  71.4 1.0 %copy.9 = bf16[4096,128]{1,0:T(8,128)(2,1)} copy(bf16[4096,128]{1,0:T(8,128)(2,1)S(1)} %mixed_rows.1) | data formatting | bytes 2097152
Async XLA Ops:
  0.0 0.7 copy-start
  0.7 0.7 copy-start.1

commit v6 on v5

--- a/solution.py
+++ b/solution.py
@@ -112,8 +112,8 @@
 
 
 def mixed_kernel(
-    lists_h, counts_h, q_h, k_h, v_h, w_h, resid_h, out,
-    lists, counts, made, came, tab, q_all, k_all, v_all, vt, s_ref, done, got, att, w_ref, stage, home, resid,
+    lists_h, q_h, k_h, v_h, w_h, resid_h, out,
+    lists, made, came, tab, q_all, k_all, v_all, vt, s_ref, done, got, att, w_ref, stage, home, resid,
     tab_sem, load_sem, out_sem, pair_send, pair_recv, q_send, q_recv, part_send, part_recv, back_send, back_recv,
 ):
     heads = lax.axis_size("head")
@@ -128,10 +128,6 @@
     in_q = pltpu.make_async_copy(q_h, q_all.at[0], load_sem.at[3])
     in_r = pltpu.make_async_copy(resid_h, resid, load_sem.at[4])
     in_l = pltpu.make_async_copy(lists_h, lists, tab_sem.at[2])
-    in_c = pltpu.make_async_copy(counts_h, counts, tab_sem.at[3])
-    for load in (in_l, in_c, in_v, in_q, in_k, load_w, in_r):
-        load.start()
-
     barrier = pltpu.get_barrier_semaphore()
     pl.semaphore_signal(barrier, inc=1, device_id=(mate, head), device_id_type=MESH)
     for i in range(heads):
@@ -140,12 +136,15 @@
         if i:
             pl.semaphore_signal(barrier, inc=1, device_id=(g, to), device_id_type=MESH)
 
+    for load in (in_l, in_v, in_q, in_k, load_w, in_r):
+        load.start()
+
     made[...] = jnp.zeros_like(made)
     in_l.wait()
-    in_c.wait()
-    used = lax.broadcasted_iota(I32, lists.shape, 0) < counts[...]
+    listed, counts = lists[0:SLOTS], lists[SLOTS : SLOTS + 1]
+    used = lax.broadcasted_iota(I32, listed.shape, 0) < counts
     for n, (first, count, base) in enumerate(((g - core, 2, 0), (cross, 1, (1 - core) * per_device))):
-        here = lists[...] - first * per_device
+        here = listed - first * per_device
         on = used & (here >= 0) & (here < count * per_device)
         made[n, 0, 0:SLOTS, 0 : lists.shape[1]] = jnp.where(on, here + base, 0)
         made[n, 1, 0:SLOTS, 0 : lists.shape[1]] = jnp.where(on, 0, 1)
@@ -233,32 +232,30 @@
             back_send.at[b, i], back_recv.at[b, i], (g, to),
         )
 
-    def project(s):
-        def join(i, carry):
-            out_part(1, s, i).wait_recv()
-            return carry
-
-        def join_own(i, carry):
-            out_part(0, s, i).wait_recv()
-            return carry
-
-        lax.fori_loop(0, heads, join, 0)
-        lax.fori_loop(0, heads - 1, join_own, 0)
-
-        for n in range(PER):
-            b = s * PER + n
-
-            def mix(source, carry):
-                att[pl.ds(b * BLK, BLK), rows(source)] = combine((got.at[0, s, source], got.at[1, s, source]), n)
-                return carry
-
-            lax.fori_loop(0, heads, mix, 0, unroll=2)
-            for c in range(0, heads, 2):
-                res = jnp.dot(att[pl.ds(b * BLK, BLK), :], w_ref[:, c * BLK : (c + 2) * BLK], preferred_element_type=F32)
-                for d in range(2):
-                    stage[c + d, pl.ds(b * BLK, BLK), :] = res[:, d * BLK : (d + 1) * BLK].astype(BF16)
-            for i in range(1, heads):
-                back(b, i).start()
+    def gather(s):
+        keep = pltpu.make_async_copy(done.at[0, head * SUBS + s], got.at[0, s, head], out_sem.at[0])
+        keep.start()
+        keep.wait()
+        for i, step in enumerate(CROSS_ORDER):
+            own = OWN_ORDER.index(step)
+            if own < heads - 1:
+                out_part(0, s, jnp.int32(own)).wait_recv()
+            out_part(1, s, jnp.int32(i)).wait_recv()
+            source = lax.rem(head // 4 + step[0], 2) * 4 + lax.rem(head % 4 - step[1] + 4, 4)
+            for n in range(PER):
+                att[pl.ds((s * PER + n) * BLK, BLK), rows(source)] = combine(
+                    (got.at[0, s, source], got.at[1, s, source]), n
+                )
+
+    def project(b):
+        for c in range(0, heads, 2):
+            res = jnp.dot(att[pl.ds(b * BLK, BLK), :], w_ref[:, c * BLK : (c + 2) * BLK], preferred_element_type=F32)
+            for d in range(2):
+                stage[c + d, pl.ds(b * BLK, BLK), :] = res[:, d * BLK : (d + 1) * BLK].astype(BF16)
+
+    def send_back(b):
+        for i in range(1, heads):
+            back(b, i).start()
 
     def pair(j, m0):
         kind, s, i = part_of(j)
@@ -272,12 +269,6 @@
         @pl.when((j > 0) & (kind1 == 0) & (i1 < heads - 1))
         def _():
             out_part(0, s1, i1).start()
-
-        @pl.when(j == 2 * heads)
-        def _():
-            keep = pltpu.make_async_copy(done.at[0, head * SUBS], got.at[0, 0, head], out_sem.at[0])
-            keep.start()
-            keep.wait()
 
         after = jnp.minimum(j + 1, turns - 1)
         kind2, s2, i2 = part_of(after)
@@ -301,8 +292,11 @@
     keep.start()
     keep.wait()
     load_w.wait()
-    project(0)
-    project(1)
+    for s in range(SUBS):
+        gather(s)
+        for n in range(PER):
+            project(s * PER + n)
+            send_back(s * PER + n)
 
     def finish(s, i):
         source = lax.rem(head - i + heads, heads)
@@ -347,7 +341,7 @@
             pltpu.make_async_copy(resid.at[where], out.at[where], out_sem.at[s * heads + i]).wait()
 
 
-def mixed_rows(lists, counts, q, k, v, w_out, resid):
+def mixed_rows(lists, q, k, v, w_out, resid):
     heads = lax.axis_size("head")
     per_device = k.shape[0]
     blocks = q.shape[0] // BLK // heads
@@ -356,11 +350,10 @@
     return pl.pallas_call(
         mixed_kernel,
         out_shape=jax.ShapeDtypeStruct(q.shape, BF16),
-        in_specs=[any_] * 7,
+        in_specs=[any_] * 6,
         out_specs=any_,
         scratch_shapes=[
             pltpu.VMEM(lists.shape, I32),
-            pltpu.VMEM(counts.shape, I32),
             pltpu.VMEM((2, 2, 16, BLK), I32),
             pltpu.VMEM((2, 16, BLK), I32),
             pltpu.SMEM((2, 2, 16, BLK), I32),
@@ -376,17 +369,18 @@
             pltpu.VMEM((heads, blocks * BLK, BLK), BF16),
             pltpu.VMEM((heads, blocks * BLK, BLK), BF16),
             pltpu.VMEM(q.shape, BF16),
-            dma((4,)), dma((5,)), dma((SUBS * heads,)), dma((3,)), dma((3,)), dma((SUBS, heads)), dma((SUBS, heads)),
+            dma((3,)), dma((5,)), dma((SUBS * heads,)), dma((3,)), dma((3,)), dma((SUBS, heads)), dma((SUBS, heads)),
             dma((2, SUBS, heads)), dma((2, SUBS, heads)), dma((blocks, heads)), dma((blocks, heads)),
         ],
         compiler_params=pltpu.CompilerParams(vmem_limit_bytes=52 << 20, collective_id=0, has_side_effects=True),
         name="mixed_rows",
-    )(lists, counts, q, k, v, w_out, resid)
+    )(lists, q, k, v, w_out, resid)
 
 
 def local(queries, resid, keys, values, w_out, block_lists, block_counts):
     keys, values = keys.reshape(-1, BLK, BLK), values.reshape(-1, BLK, BLK)
-    return mixed_rows(block_lists.T, block_counts[None, :], queries, keys, values, w_out, resid)
+    lists = jnp.concatenate([block_lists.T, block_counts[None, :]], axis=0)
+    return mixed_rows(lists, queries, keys, values, w_out, resid)
 
 
 def solution(mesh):

time: 72.8 us -> 72.3 us (level)
  local copies, waits for them, and re-layouts: 2.32 us -> 0.97 us
    unnamed x5 -> x1, local copies, waits for them, and re-layouts: 2.32 us -> 0.97 us
where the time goes in v6:
time: 72.3 us; the launch traced here: 71.3 us
  Pallas kernels  69.6 us (96%)
  local copies, waits for them, and re-layouts  0.97 us (1%)
    pallas_call x1, Pallas kernels, mixed_rows(): pl.pallas_call(mixed_kernel, out_shape=jax.ShapeDtypeStruct(q.shape, BF16...  69.6 us

profile of v6, /device:TPU:24, one launch (start us, length us, event | category | flops | bytes accessed | tf_op | source)
XLA Modules:
  0.0 71.3 jit_solution(17501819227700611028)
XLA Ops:
  0.0 0.7 %pad_add_fusion.lists_h = s32[13,32]{1,0:T(8,128)S(1)} fusion(s32[1,32]{1,0:T(1,128)} %bitcast.7, s32[12,32]{1,0:T(8,128)} %bitcast.6), kind=kLoop, calls=%fused_computation | loop fusion | flops 416 | bytes 3328 | tf_op jit(solution)/shard_map/concatenate | solution.py:382
  0.7 69.6 %mixed_rows.1 = bf16[4096,128]{1,0:T(8,128)(2,1)S(1)} custom-call(s32[13,32]{1,0:T(8,128)S(1)} %pad_add_fusion.lists_h, bf16[4096,128]{1,0:T(8,128)(2,1)} %q_h.1, bf16[48,128,128]{2,1,0:T(8,128)(2,1)} %bitcast.4, bf16[48,128,128]{2,1,0:T(8,128)(2,1)} %bitcast.5, bf16[1024,1024]{1,0:T(8,128)(2,1)} %w_h.1, bf16[4096,128]{1,0:T(8,128)(2,1)} %resid_h.1), custom_call_target="tpu_custom_call" | custom-call | tf_op jit(solution)/shard_map/mixed_rows/pallas_call | solution.py:350
  70.3 1.0 %copy.9 = bf16[4096,128]{1,0:T(8,128)(2,1)} copy(bf16[4096,128]{1,0:T(8,128)(2,1)S(1)} %mixed_rows.1) | data formatting | bytes 2097152

commit v7 on v6

--- a/solution.py
+++ b/solution.py
@@ -170,14 +170,16 @@
     out_v = remote(v_h, v_all.at[mine], pair_send.at[1], pair_recv.at[1], (mate, head))
     out_k = remote(k_h, k_all.at[mine], pair_send.at[2], pair_recv.at[2], (mate, head))
     out_t.start()
+
+    def send_q(i, s):
+        out_q(s, i).start()
+        return s
+
+    lax.fori_loop(0, 2, send_q, jnp.int32(0))
     out_v.start()
     out_k.start()
-    for s in range(SUBS):
-        def send_q(i, carry):
-            out_q(s, i).start()
-            return carry
-
-        lax.fori_loop(0, heads, send_q, 0)
+    lax.fori_loop(2, heads, send_q, jnp.int32(0))
+    lax.fori_loop(0, heads, send_q, jnp.int32(1))
     in_v.wait()
     turn_values(v_all, vt, core * per_device, per_device)
     out_t.wait_recv()
@@ -298,23 +300,21 @@
             project(s * PER + n)
             send_back(s * PER + n)
 
-    def finish(s, i):
+    def keep_rows(b, i):
         source = lax.rem(head - i + heads, heads)
-        where = rows(source * SUBS + s, size)
-        if i:
-            for n in range(PER):
-                back(s * PER + n, i).wait_recv()
-            come = home[source, pl.ds(s * size, size), :]
-        else:
-            come = stage[head, pl.ds(s * size, size), :]
-        resid[where, :] = (resid[where, :].astype(F32) + come.astype(F32)).astype(BF16)
-        return pltpu.make_async_copy(resid.at[where], out.at[where], out_sem.at[s * heads + i])
+        where = rows(source * blocks + b)
+        return source, where, pltpu.make_async_copy(resid.at[where], out.at[where], out_sem.at[b * heads + i])
 
     in_r.wait()
-    for s in range(SUBS):
+    for b in range(blocks):
         for i in range(heads):
-            finish_copy = finish(s, i)
-            finish_copy.start()
+            source, where, keep = keep_rows(b, i)
+            part = pl.ds(b * BLK, BLK)
+            if i:
+                back(b, i).wait_recv()
+            come = home[source, part, :] if i else stage[head, part, :]
+            resid[where, :] = (resid[where, :].astype(F32) + come.astype(F32)).astype(BF16)
+            keep.start()
 
     out_t.wait_send()
     out_v.wait_send()
@@ -332,13 +332,11 @@
 
         lax.fori_loop(0, heads, sent, 0)
         lax.fori_loop(0, heads - 1, sent_own, 0)
+    for b in range(blocks):
         for i in range(heads):
             if i:
-                for n in range(PER):
-                    back(s * PER + n, i).wait_send()
-            source = lax.rem(head - i + heads, heads)
-            where = rows(source * SUBS + s, size)
-            pltpu.make_async_copy(resid.at[where], out.at[where], out_sem.at[s * heads + i]).wait()
+                back(b, i).wait_send()
+            keep_rows(b, i)[2].wait()
 
 
 def mixed_rows(lists, q, k, v, w_out, resid):
@@ -369,7 +367,7 @@
             pltpu.VMEM((heads, blocks * BLK, BLK), BF16),
             pltpu.VMEM((heads, blocks * BLK, BLK), BF16),
             pltpu.VMEM(q.shape, BF16),
-            dma((3,)), dma((5,)), dma((SUBS * heads,)), dma((3,)), dma((3,)), dma((SUBS, heads)), dma((SUBS, heads)),
+            dma((3,)), dma((5,)), dma((blocks * heads,)), dma((3,)), dma((3,)), dma((SUBS, heads)), dma((SUBS, heads)),
             dma((2, SUBS, heads)), dma((2, SUBS, heads)), dma((blocks, heads)), dma((blocks, heads)),
         ],
         compiler_params=pltpu.CompilerParams(vmem_limit_bytes=52 << 20, collective_id=0, has_side_effects=True),

time: 72.3 us -> 72.5 us (level)
  no operation moved by 1% of the time
where the time goes in v7:
time: 72.5 us; the launch traced here: 71.2 us
  Pallas kernels  69.4 us (96%)
  local copies, waits for them, and re-layouts  0.97 us (1%)
    pallas_call x1, Pallas kernels, mixed_rows(): pl.pallas_call(mixed_kernel, out_shape=jax.ShapeDtypeStruct(q.shape, BF16...  69.4 us

profile of v7, /device:TPU:24, one launch (start us, length us, event | category | flops | bytes accessed | tf_op | source)
XLA Modules:
  0.0 71.2 jit_solution(13713228715557426801)
XLA Ops:
  0.0 0.7 %pad_add_fusion.lists_h = s32[13,32]{1,0:T(8,128)S(1)} fusion(s32[1,32]{1,0:T(1,128)} %bitcast.7, s32[12,32]{1,0:T(8,128)} %bitcast.6), kind=kLoop, calls=%fused_computation | loop fusion | flops 416 | bytes 3328 | tf_op jit(solution)/shard_map/concatenate | solution.py:380
  0.7 69.4 %mixed_rows.1 = bf16[4096,128]{1,0:T(8,128)(2,1)S(1)} custom-call(s32[13,32]{1,0:T(8,128)S(1)} %pad_add_fusion.lists_h, bf16[4096,128]{1,0:T(8,128)(2,1)} %q_h.1, bf16[48,128,128]{2,1,0:T(8,128)(2,1)} %bitcast.4, bf16[48,128,128]{2,1,0:T(8,128)(2,1)} %bitcast.5, bf16[1024,1024]{1,0:T(8,128)(2,1)} %w_h.1, bf16[4096,128]{1,0:T(8,128)(2,1)} %resid_h.1), custom_call_target="tpu_custom_call" | custom-call | tf_op jit(solution)/shard_map/mixed_rows/pallas_call | solution.py:348
  70.2 1.0 %copy.9 = bf16[4096,128]{1,0:T(8,128)(2,1)} copy(bf16[4096,128]{1,0:T(8,128)(2,1)S(1)} %mixed_rows.1) | data formatting | bytes 2097152
